TPU v7x, 32 devices: a whole 2x2x4 slice. The times are simulated.
32 devices in a mesh: blk: 8 (over z, x), rep: 4 (over y, core).
Axes of the slice: x: 2, y: 2, z: 4, core: 2. Of those that a mesh axis runs over, the one named last changes fastest.
Arguments:
- hidden: bfloat16 [4, 8, 256, 768], P('rep', 'blk'), may hold values from -6 to 6
- store: bfloat16 [4, 128, 768], P('rep', 'blk'), may hold values from -6 to 6
- retrieved: int32 [4, 8, 256, 64], P('rep', 'blk'), may hold values from 0 to 127, as said below
- live: int32 [4, 8, 256, 64], P('rep', 'blk'), may hold values 0 or 1
- lengths: int32 [4, 8], P('rep', 'blk'), may hold values from 64 to 256, as said below
- self_qkv: bfloat16 [768, 2304], replicated, may hold values from -0.21875 to 0.21875
- self_bias: float32 [2, 768], replicated, may hold values from -0.6 to 0.6
- self_out: bfloat16 [768, 768], replicated, may hold values from -1.75 to 1.75
- self_out_bias: float32 [768], replicated, may hold values from -0.6 to 0.6
- norm1: float32 [2, 768], replicated, may hold values from -0.3 to 1.3, as said below
- cross_q: bfloat16 [768, 768], replicated, may hold values from -0.21875 to 0.21875
- cross_q_bias: float32 [768], replicated, may hold values from -0.6 to 0.6
- cross_kv: bfloat16 [768, 1536], replicated, may hold values from -0.21875 to 0.21875
- cross_v_bias: float32 [768], replicated, may hold values from -0.6 to 0.6
- cross_out: bfloat16 [768, 768], replicated, may hold values from -1.75 to 1.75
- cross_out_bias: float32 [768], replicated, may hold values from -0.6 to 0.6
- norm2: float32 [2, 768], replicated, may hold values from -0.3 to 1.3, as said below
- ffn_in: bfloat16 [768, 3072], replicated, may hold values from -0.21875 to 0.21875
- ffn_in_bias: float32 [3072], replicated, may hold values from -0.6 to 0.6
- ffn_out: bfloat16 [3072, 768], replicated, may hold values from -0.109375 to 0.109375
- ffn_out_bias: float32 [768], replicated, may hold values from -0.6 to 0.6
- norm3: float32 [2, 768], replicated, may hold values from -0.3 to 1.3, as said below
- cotangent: bfloat16 [4, 8, 256, 768], P('rep', 'blk'), may hold values from -6 to 6
Outputs:
- output: bfloat16 [4, 8, 256, 768], P('rep', 'blk')
- d_hidden: float32 [4, 8, 256, 768], P('rep', 'blk')
- d_store: float32 [4, 128, 768], P('rep', 'blk')
- d_self_qkv: float32 [768, 2304], P('blk')
- d_self_bias: float32 [2, 768], P(None, 'blk')
- d_self_out: float32 [768, 768], P('blk')
- d_self_out_bias: float32 [768], P('blk')
- d_norm1: float32 [2, 768], P(None, 'blk')
- d_cross_q: float32 [768, 768], P('blk')
- d_cross_q_bias: float32 [768], P('blk')
- d_cross_kv: float32 [768, 1536], P('blk')
- d_cross_v_bias: float32 [768], P('blk')
- d_cross_out: float32 [768, 768], P('blk')
- d_cross_out_bias: float32 [768], P('blk')
- d_norm2: float32 [2, 768], P(None, 'blk')
- d_ffn_in: float32 [768, 3072], P('blk')
- d_ffn_in_bias: float32 [3072], P('blk')
- d_ffn_out: float32 [3072, 768], P('blk')
- d_ffn_out_bias: float32 [768], P('blk')
- d_norm3: float32 [2, 768], P(None, 'blk')
Inputs may be any that keep to these rules, and one draw needn't show every extreme that they name: `retrieved`: each query names 64 different slots: one in each of 64 cyclic runs of 2 consecutive slots that start at a shift of the query's own. `lengths`: in each group one summary has exactly 64 tokens and another exactly 256; rows at or past a summary's length are padding. `norm1`: row 0 is a gain, row 1 a shift. `norm2`: row 0 is a gain, row 1 a shift. `norm3`: row 0 is a gain, row 1 a shift.
All inputs are finite; a program needn't handle non-finite values. No bound on the sum of `live` on one device may be relied on, other than what follows from the above.
Results may differ from a plain program's by a relative error of at most 0.025.
Values may be sent and summed in bfloat16 or wider, within the bound.
A program may use at most 192 MiB of HBM per device.

v0:
```python
import math

import jax
import jax.numpy as jnp
from jax import lax
from jax.sharding import PartitionSpec as P

D = 768
HEADS = 12
HD = 64


EPS = 1e-05
NEG = -1e30
HIGH = lax.Precision.HIGHEST


def split_up(value, dim, count):
    shape = value.shape
    parts = value.reshape(*shape[:dim], count, shape[dim] // count, *shape[dim + 1 :])
    return jnp.moveaxis(parts, dim, 0)


def sum_at_owner(value, axis, dim):
    count = lax.axis_size(axis)
    parts = lax.all_to_all(split_up(value, dim, count), axis, 0, 0, tiled=True)
    return jnp.sum(parts.astype(jnp.float32), axis=0)


def side_by_side(arrays, axis, dim, along):
    both = jnp.concatenate(arrays, axis=along)
    whole, at, finished = (sum_at_owner(both, axis, dim), 0, [])
    for a in arrays:
        finished.append(lax.slice_in_dim(whole, at, at + a.shape[along], axis=along))
        at += a.shape[along]
    return tuple(finished)


def layer_norm(resid_in, norm_params):
    mean_val = jnp.mean(resid_in, axis=-1, keepdims=True)
    centered = resid_in - mean_val
    variance = jnp.mean(centered * centered, axis=-1, keepdims=True)
    return centered * lax.rsqrt(variance + EPS) * norm_params[0] + norm_params[1]


def matmul(left_op, right_op):
    return jnp.dot(left_op, right_op, preferred_element_type=jnp.float32)


def matmul_tn(left_op, right_op):
    return lax.dot_general(
        left_op, right_op, (((0,), (0,)), ((), ())), preferred_element_type=jnp.float32
    )


def matmul_nt(left_op, right_op):
    return lax.dot_general(
        left_op, right_op, (((1,), (1,)), ((), ())), preferred_element_type=jnp.float32
    )


def exact_tn(left_op, right_op):
    return lax.dot_general(
        left_op,
        right_op,
        (((0,), (0,)), ((), ())),
        precision=HIGH,
        preferred_element_type=jnp.float32,
    )


def exact_nt(left_op, right_op):
    return lax.dot_general(
        left_op,
        right_op,
        (((1,), (1,)), ((), ())),
        precision=HIGH,
        preferred_element_type=jnp.float32,
    )


def col_sum(values):
    return jnp.sum(values.astype(jnp.float32), axis=0)


def split_heads(values):
    return values.reshape(values.shape[0], HEADS, HD)


def exact_gelu(values):
    return jax.nn.gelu(values, approximate=False)


def cross_piece(carry, piece, queries, store_mask, scaling):
    key_rows, value_rows = piece
    piece_len = key_rows.shape[0]
    step_len = math.gcd(piece_len, 512)
    q_heads = split_heads(queries)

    def one_step(index, state):
        top_old, total_old, acc_old = state
        offset = index * step_len
        key_block = lax.dynamic_slice_in_dim(key_rows, offset, step_len, 0)
        value_block = lax.dynamic_slice_in_dim(value_rows, offset, step_len, 0)
        allowed = lax.dynamic_slice_in_dim(store_mask, offset, step_len, 1)
        raw_scores = jnp.einsum(
            "qhd,khd->hqk", q_heads, split_heads(key_block), preferred_element_type=jnp.float32
        )
        scores = jnp.where(allowed[None], raw_scores * scaling, NEG)
        top_new = jnp.maximum(top_old, jnp.max(scores, axis=-1, keepdims=True))
        exp_scores = jnp.where(allowed[None], jnp.exp(scores - top_new), 0.0)
        fade_factor = jnp.exp(top_old - top_new)
        total_new = total_old * fade_factor + jnp.sum(exp_scores, axis=-1, keepdims=True)
        acc_new = acc_old * fade_factor + jnp.einsum(
            "hqk,khd->hqd",
            exp_scores.astype(jnp.bfloat16),
            split_heads(value_block),
            preferred_element_type=jnp.float32,
        )
        return (top_new, total_new, acc_new)

    return lax.fori_loop(0, piece_len // step_len, one_step, carry)


def self_allowed(begin, finish, length):
    places_q = jnp.arange(begin, finish, dtype=jnp.int32)
    places_k = jnp.arange(finish, dtype=jnp.int32)
    return (places_k[None, :] <= places_q[:, None]) & (places_k[None, :] < length)


def self_forward(queries, key_rows, value_rows, length, scaling):
    seq_len = queries.shape[0]
    step_len = math.gcd(seq_len, 512)
    allowed = self_allowed(0, step_len, length)
    raw_scores = jnp.einsum(
        "qhd,khd->hqk",
        split_heads(queries),
        split_heads(key_rows),
        preferred_element_type=jnp.float32,
    )
    scores = jnp.where(allowed[None], raw_scores * scaling, NEG)
    top_val = jnp.max(scores, axis=-1, keepdims=True)
    exp_scores = jnp.exp(scores - top_val)
    total_val = jnp.sum(exp_scores, axis=-1, keepdims=True)
    weights = (exp_scores / total_val).astype(jnp.bfloat16)
    mixed = jnp.einsum(
        "hqk,khd->qhd", weights, split_heads(value_rows), preferred_element_type=jnp.float32
    )
    mixed_parts = mixed.reshape(step_len, HEADS * HD)
    lse_parts = top_val + jnp.log(total_val)
    return (mixed_parts, lse_parts)


def attend_back(queries, key_rows, value_rows, allowed, lse_rows, delta, grad_mix, scaling):
    q_heads = split_heads(queries)
    k_heads = split_heads(key_rows)
    v_heads = split_heads(value_rows)
    g_heads = split_heads(grad_mix)
    raw_scores = jnp.einsum("qhd,khd->hqk", q_heads, k_heads, preferred_element_type=jnp.float32)
    scores = jnp.where(allowed[None], raw_scores * scaling, NEG)
    probs = jnp.where(allowed[None], jnp.exp(scores - lse_rows), 0.0)
    grad_values = jnp.einsum(
        "hqk,qhd->khd", probs.astype(jnp.bfloat16), g_heads, preferred_element_type=jnp.float32
    )
    grad_probs = jnp.einsum("qhd,khd->hqk", g_heads, v_heads, preferred_element_type=jnp.float32)
    if delta is None:
        delta = jnp.sum(probs * grad_probs, axis=-1, keepdims=True)
    grad_scores = (probs * (grad_probs - delta)).astype(jnp.bfloat16)
    grad_query = (
        jnp.einsum("hqk,khd->qhd", grad_scores, k_heads, preferred_element_type=jnp.float32)
        * scaling
    )
    grad_keys = (
        jnp.einsum("hqk,qhd->khd", grad_scores, q_heads, preferred_element_type=jnp.float32)
        * scaling
    )
    return (
        grad_query.reshape(queries.shape[0], HEADS * HD),
        grad_keys.reshape(key_rows.shape[0], HEADS * HD),
        grad_values.reshape(key_rows.shape[0], HEADS * HD),
    )


def self_backward(queries, key_rows, value_rows, length, lse_all, grad_mix, scaling):
    seq_len, width = queries.shape
    step_len = math.gcd(seq_len, 512)
    allowed = self_allowed(0, step_len, length)
    part_q, part_k, part_v = attend_back(
        queries, key_rows, value_rows, allowed, lse_all, None, grad_mix, scaling
    )
    return (part_q, part_k, part_v)


def owner_grads(home_keys, home_values, states, cross_kv_f):
    home_all = jnp.concatenate([home_keys, home_values], axis=1)
    d_store = exact_nt(home_all, cross_kv_f)
    d_cross_kv = exact_tn(states.astype(jnp.float32), home_all)
    return (d_store, d_cross_kv, jnp.sum(home_values, axis=0))


def on_device(
    hidden,
    store,
    retrieved,
    live,
    lengths,
    self_qkv,
    self_bias,
    self_out,
    self_out_bias,
    norm1,
    cross_q,
    cross_q_bias,
    cross_kv,
    cross_v_bias,
    cross_out,
    cross_out_bias,
    norm2,
    ffn_in,
    ffn_in_bias,
    ffn_out,
    ffn_out_bias,
    norm3,
    cotangent,
):
    tokens = hidden[0, 0]
    seq_len = tokens.shape[0]
    scaling = HD ** (-0.5)
    length = lengths[0, 0]
    states = store[0]
    slots_total = states.shape[0] * lax.axis_size("blk")
    tokens_f = tokens.astype(jnp.float32)
    projected = matmul(tokens, self_qkv)
    queries = (projected[:, :D] + self_bias[0]).astype(jnp.bfloat16)
    key_rows = projected[:, D : 2 * D].astype(jnp.bfloat16)
    value_rows = (projected[:, 2 * D :] + self_bias[1]).astype(jnp.bfloat16)
    self_mix, self_lse = self_forward(queries, key_rows, value_rows, length, scaling)
    self_mix_b = self_mix.astype(jnp.bfloat16)
    first_res = tokens_f + matmul(self_mix_b, self_out) + self_out_bias
    first = layer_norm(first_res, norm1)
    first_b = first.astype(jnp.bfloat16)
    cross_query = (matmul(first_b, cross_q) + cross_q_bias).astype(jnp.bfloat16)
    chosen = retrieved[0, 0]
    usable = (live[0, 0] > 0) | (jnp.arange(chosen.shape[1], dtype=jnp.int32) == 0)[None, :]
    row_ids = jnp.arange(seq_len, dtype=jnp.int32)[:, None]
    store_mask = jnp.zeros((seq_len, slots_total), jnp.bool_).at[row_ids, chosen].set(usable)
    initial = (
        jnp.full((HEADS, seq_len, 1), NEG, jnp.float32),
        jnp.zeros((HEADS, seq_len, 1), jnp.float32),
        jnp.zeros((HEADS, seq_len, HD), jnp.float32),
    )
    store_proj = matmul(states, cross_kv)
    store_keys = store_proj[:, :D].astype(jnp.bfloat16)
    store_values = (store_proj[:, D:] + cross_v_bias).astype(jnp.bfloat16)
    cross_state = cross_piece(
        initial,
        (
            lax.all_gather(store_keys, "blk", axis=0, tiled=True),
            lax.all_gather(store_values, "blk", axis=0, tiled=True),
        ),
        cross_query,
        store_mask,
        scaling,
    )
    top_run, total_run, acc_run = cross_state
    cross_mix = (acc_run / total_run).transpose(1, 0, 2).reshape(seq_len, D)
    cross_lse = top_run + jnp.log(total_run)
    cross_mix_b = cross_mix.astype(jnp.bfloat16)
    second_res = first + matmul(cross_mix_b, cross_out) + cross_out_bias
    second = layer_norm(second_res, norm2)
    second_b = second.astype(jnp.bfloat16)
    inner = matmul(second_b, ffn_in) + ffn_in_bias
    activated = exact_gelu(inner).astype(jnp.bfloat16)
    third_res = second + matmul(activated, ffn_out) + ffn_out_bias
    result = layer_norm(third_res, norm3)
    row_live = (jnp.arange(seq_len, dtype=jnp.int32) < length).astype(jnp.float32)[:, None]
    grad_out = cotangent[0, 0].astype(jnp.float32) * row_live
    _, pull_third = jax.vjp(layer_norm, third_res, norm3)
    d_third, d_norm3 = pull_third(grad_out)
    d_fb = d_third.astype(jnp.bfloat16)
    d_ffn_out = matmul_tn(activated, d_fb)
    d_ffn_out_bias = col_sum(d_fb)
    _, pull_gelu = jax.vjp(exact_gelu, inner)
    d_inner = pull_gelu(matmul_nt(d_fb, ffn_out))[0].astype(jnp.bfloat16)
    d_ffn_in = matmul_tn(second_b, d_inner)
    d_ffn_in_bias = col_sum(d_inner)
    d_second = d_third + matmul_nt(d_inner, ffn_in)
    _, pull_second = jax.vjp(layer_norm, second_res, norm2)
    d_second_res, d_norm2 = pull_second(d_second)
    d_cb = d_second_res.astype(jnp.bfloat16)
    d_cross_out = matmul_tn(cross_mix_b, d_cb)
    d_cross_out_bias = col_sum(d_cb)
    vectors_a = jnp.stack(
        [d_ffn_out_bias, d_norm3[0], d_norm3[1], d_norm2[0], d_norm2[1], d_cross_out_bias], axis=1
    )
    d_cross_mix = matmul_nt(d_cb, cross_out).astype(jnp.bfloat16)
    delta_cross = jnp.sum(
        split_heads(d_cross_mix.astype(jnp.float32) * cross_mix), axis=-1
    ).transpose(1, 0)[:, :, None]
    back_keys, back_values = (
        lax.all_gather(store_keys, "blk", axis=0, tiled=True),
        lax.all_gather(store_values, "blk", axis=0, tiled=True),
    )
    slot_step = math.gcd(slots_total, 512)

    def slot_block(query_acc, index):
        offset = index * slot_step
        key_block = lax.dynamic_slice_in_dim(back_keys, offset, slot_step, 0)
        value_block = lax.dynamic_slice_in_dim(back_values, offset, slot_step, 0)
        allowed = lax.dynamic_slice_in_dim(store_mask, offset, slot_step, 1)
        part_q, part_k, part_v = attend_back(
            cross_query,
            key_block,
            value_block,
            allowed,
            cross_lse,
            delta_cross,
            d_cross_mix,
            scaling,
        )
        return (query_acc + part_q, (part_k, part_v))

    d_cross_query, (key_terms, value_terms) = lax.scan(
        slot_block,
        jnp.zeros((seq_len, D), jnp.float32),
        jnp.arange(slots_total // slot_step, dtype=jnp.int32),
    )
    key_terms = key_terms.reshape(slots_total, D)
    value_terms = value_terms.reshape(slots_total, D)
    cross_kv_f = cross_kv.astype(jnp.float32)
    home_keys, home_values = side_by_side(
        (key_terms.astype(jnp.bfloat16), value_terms.astype(jnp.bfloat16)), "blk", 0, 1
    )
    d_store, d_cross_kv, d_cross_v_bias = owner_grads(home_keys, home_values, states, cross_kv_f)
    d_cq = d_cross_query.astype(jnp.bfloat16)
    d_cross_q = matmul_tn(first_b, d_cq)
    d_cross_q_bias = col_sum(d_cq)
    d_first = d_second_res + matmul_nt(d_cq, cross_q)
    _, pull_first = jax.vjp(layer_norm, first_res, norm1)
    d_first_res, d_norm1 = pull_first(d_first)
    d_sb = d_first_res.astype(jnp.bfloat16)
    d_self_out = matmul_tn(self_mix_b, d_sb)
    d_self_out_bias = col_sum(d_sb)
    d_self_mix = matmul_nt(d_sb, self_out).astype(jnp.bfloat16)
    grad_query, grad_keys, grad_values = self_backward(
        queries, key_rows, value_rows, length, self_lse, d_self_mix, scaling
    )
    d_projected = jnp.concatenate([grad_query, grad_keys, grad_values], axis=1).astype(jnp.bfloat16)
    d_self_qkv = matmul_tn(tokens, d_projected)
    d_hidden = d_first_res + matmul_nt(d_projected, self_qkv)
    vectors_b = jnp.stack(
        [
            col_sum(d_projected[:, :D]),
            col_sum(d_projected[:, 2 * D :]),
            d_self_out_bias,
            d_norm1[0],
            d_norm1[1],
            d_cross_q_bias,
            d_cross_v_bias,
        ],
        axis=1,
    )
    (
        g_ffn_in,
        g_ffn_out,
        g_cross_out,
        g_ffn_in_bias,
        g_vectors_a,
        g_self_qkv,
        g_self_out,
        g_cross_q,
        g_cross_kv,
        g_vectors_b,
    ) = (
        lax.psum_scatter(d_ffn_in, "blk", scatter_dimension=0, tiled=True),
        lax.psum_scatter(d_ffn_out, "blk", scatter_dimension=0, tiled=True),
        lax.psum_scatter(d_cross_out, "blk", scatter_dimension=0, tiled=True),
        lax.psum_scatter(d_ffn_in_bias, "blk", scatter_dimension=0, tiled=True),
        lax.psum_scatter(vectors_a, "blk", scatter_dimension=0, tiled=True),
        lax.psum_scatter(d_self_qkv, "blk", scatter_dimension=0, tiled=True),
        lax.psum_scatter(d_self_out, "blk", scatter_dimension=0, tiled=True),
        lax.psum_scatter(d_cross_q, "blk", scatter_dimension=0, tiled=True),
        lax.psum_scatter(d_cross_kv, "blk", scatter_dimension=0, tiled=True),
        lax.psum_scatter(vectors_b, "blk", scatter_dimension=0, tiled=True),
    )
    (
        g_ffn_in,
        g_ffn_out,
        g_cross_out,
        g_ffn_in_bias,
        g_vectors_a,
        g_self_qkv,
        g_self_out,
        g_cross_q,
        g_cross_kv,
        g_vectors_b,
    ) = (
        lax.psum(g_ffn_in.astype(jnp.bfloat16), "rep").astype(jnp.float32),
        lax.psum(g_ffn_out.astype(jnp.bfloat16), "rep").astype(jnp.float32),
        lax.psum(g_cross_out.astype(jnp.bfloat16), "rep").astype(jnp.float32),
        lax.psum(g_ffn_in_bias.astype(jnp.bfloat16), "rep").astype(jnp.float32),
        lax.psum(g_vectors_a.astype(jnp.bfloat16), "rep").astype(jnp.float32),
        lax.psum(g_self_qkv.astype(jnp.bfloat16), "rep").astype(jnp.float32),
        lax.psum(g_self_out.astype(jnp.bfloat16), "rep").astype(jnp.float32),
        lax.psum(g_cross_q.astype(jnp.bfloat16), "rep").astype(jnp.float32),
        lax.psum(g_cross_kv.astype(jnp.bfloat16), "rep").astype(jnp.float32),
        lax.psum(g_vectors_b.astype(jnp.bfloat16), "rep").astype(jnp.float32),
    )
    return (
        result.astype(jnp.bfloat16)[None, None],
        d_hidden[None, None],
        d_store[None],
        g_self_qkv,
        jnp.stack([g_vectors_b[:, 0], g_vectors_b[:, 1]]),
        g_self_out,
        g_vectors_b[:, 2],
        jnp.stack([g_vectors_b[:, 3], g_vectors_b[:, 4]]),
        g_cross_q,
        g_vectors_b[:, 5],
        g_cross_kv,
        g_vectors_b[:, 6],
        g_cross_out,
        g_vectors_a[:, 5],
        jnp.stack([g_vectors_a[:, 3], g_vectors_a[:, 4]]),
        g_ffn_in,
        g_ffn_in_bias,
        g_ffn_out,
        g_vectors_a[:, 0],
        jnp.stack([g_vectors_a[:, 1], g_vectors_a[:, 2]]),
    )


def solution(mesh):
    in_specs = (
        P("rep", "blk", None, None),
        P("rep", "blk", None),
        P("rep", "blk", None, None),
        P("rep", "blk", None, None),
        P("rep", "blk"),
        P(),
        P(),
        P(),
        P(),
        P(),
        P(),
        P(),
        P(),
        P(),
        P(),
        P(),
        P(),
        P(),
        P(),
        P(),
        P(),
        P(),
        P("rep", "blk", None, None),
    )
    out_specs = (
        P("rep", "blk", None, None),
        P("rep", "blk", None, None),
        P("rep", "blk", None),
        P("blk", None),
        P(None, "blk"),
        P("blk", None),
        P("blk"),
        P(None, "blk"),
        P("blk", None),
        P("blk"),
        P("blk", None),
        P("blk"),
        P("blk", None),
        P("blk"),
        P(None, "blk"),
        P("blk", None),
        P("blk"),
        P("blk", None),
        P("blk"),
        P(None, "blk"),
    )
    return jax.shard_map(
        on_device, mesh=mesh, in_specs=in_specs, out_specs=out_specs, check_vma=False
    )
```

profile of v0, /device:TPU:0, one launch (start us, length us, event | category | flops | bytes accessed | tf_op | source)
XLA Modules:
  0.0 1229.4 jit_solution(14988443939161093898)
XLA Ops:
  40.1 69.3 %scatter_custom_fusion = pred[32768]{0:T(1024)(128)(4,1)} fusion(s32[16384]{0:T(1024)} %reshape.365, pred[16384]{0:T(1024)(128)(4,1)} %reshape.367, pred[]{:T(512)} %constant.46.clone.1), kind=kCustom, calls=%fused_computation.132 | custom fusion | bytes 33280
  113.7 34.4 %all_gather.8 = bf16[128,768]{1,0:T(8,128)(2,1)} all-gather(bf16[16,768]{1,0:T(8,128)(2,1)S(1)} %slice.217), channel_id=1, replica_groups=mesh['blk'=8,'rep'=4] {'blk'}, dimensions={0}, use_global_device_ids=true | all-gather | bytes 221184 | tf_op jit(solution)/shard_map/all_gather | solution.py:258
  155.6 33.0 %all_gather.9 = bf16[128,768]{1,0:T(8,128)(2,1)} all-gather(bf16[16,768]{1,0:T(8,128)(2,1)S(1)} %fusion.60), channel_id=1, replica_groups=mesh['blk'=8,'rep'=4] {'blk'}, dimensions={0}, use_global_device_ids=true | all-gather | bytes 221184 | tf_op jit(solution)/shard_map/all_gather | solution.py:259
  199.0 9.8 multiply_convert_fusion.1
  262.3 14.8 %all_to_all.5 = bf16[8,16,1536]{2,1,0:T(8,128)(2,1)S(1)} all-to-all(bf16[8,16,1536]{2,1,0:T(8,128)(2,1)S(1)} %pad_maximum_fusion.3), channel_id=1, replica_groups=mesh['blk'=8,'rep'=4] {'blk'}, dimensions={0} | all-to-all | bytes 786432 | tf_op jit(solution)/shard_map/all_to_all | solution.py:26
  277.8 4.9 convolution_bitcast_fusion.1
  282.8 6.1 copy.161
  301.5 4.0 convolution_bitcast_fusion
  305.5 8.0 copy.157
  314.2 6.9 fusion.87
  321.4 6.6 fusion.102
  348.9 32.1 %reduce-scatter.18.cloned.1.call-done = f32[96,768]{1,0:T(8,128)} async-done(((f32[768,768]{1,0:T(8,128)}), f32[96,768]{1,0:T(8,128)}) %reduce-scatter.18.cloned.1.call-update) | async-done | bytes 294928 | tf_op jit(solution)/shard_map/reduce_scatter | solution.py:381
  382.6 69.9 %reduce-scatter.22.cloned.1.call-done = f32[96,768]{1,0:T(8,128)} async-done(((f32[768,768]{1,0:T(8,128)}), f32[96,768]{1,0:T(8,128)}) %reduce-scatter.22.cloned.1.call-update) | async-done | bytes 294928 | tf_op jit(solution)/shard_map/reduce_scatter | solution.py:377
  454.1 96.4 %reduce-scatter.32.cloned.1.call-done = f32[96,1536]{1,0:T(8,128)} async-done(((f32[768,1536]{1,0:T(8,128)}), f32[96,1536]{1,0:T(8,128)}) %reduce-scatter.32.cloned.1.call-update) | async-done | bytes 589840
  552.6 130.3 %reduce-scatter.28.cloned.1.call-done = f32[96,2304]{1,0:T(8,128)} async-done(((f32[768,2304]{1,0:T(8,128)}), f32[96,2304]{1,0:T(8,128)}) %reduce-scatter.28.cloned.1.call-update) | async-done | bytes 884752
  685.1 164.2 %reduce-scatter.24.cloned.1.call-done = f32[96,3072]{1,0:T(8,128)} async-done(((f32[768,3072]{1,0:T(8,128)}), f32[96,3072]{1,0:T(8,128)}) %reduce-scatter.24.cloned.1.call-update) | async-done | bytes 1179664 | tf_op jit(solution)/shard_map/reduce_scatter | solution.py:375
  851.5 164.5 %reduce-scatter.26.cloned.1.call-done = f32[384,768]{1,0:T(8,128)} async-done(((f32[3072,768]{1,0:T(8,128)}), f32[384,768]{1,0:T(8,128)}) %reduce-scatter.26.cloned.1.call-update) | async-done | bytes 1179664 | tf_op jit(solution)/shard_map/reduce_scatter | solution.py:376
  1018.1 3.5 fusion.18
  1023.5 35.2 %all-reduce.6 = bf16[3072]{0:T(1024)(128)(2,1)} all-reduce(f32[3072]{0:T(1024)S(1)} %copy-done.54), channel_id=10, replica_groups=mesh['blk'=8,'rep'=4] {'blk'}, use_global_device_ids=true, to_apply=%region_50.51.clone | all-reduce | flops 3072 | bytes 18432
  1059.4 20.7 %reduce-scatter.34.cloned.1.call-done = f32[96,6]{1,0:T(8,128)} async-done(((f32[768,6]{1,0:T(8,128)}), f32[96,6]{1,0:T(8,128)}) %reduce-scatter.34.cloned.1.call-update) | async-done | bytes 2320
  1081.0 4.3 convolution_bitcast_fusion.3
  1085.3 58.9 %reduce-scatter.30.cloned.1.call-done = f32[96,7]{1,0:T(8,128)} async-done(((f32[768,7]{1,0:T(8,128)}), f32[96,7]{1,0:T(8,128)}) %reduce-scatter.30.cloned.1.call-update) | async-done | bytes 2704
  1145.1 6.3 all-reduce.7
  1156.7 52.2 %all-reduce.11.cloned.1.call-done = (bf16[96,2304]{0,1:T(8,128)(2,1)}, bf16[96,1536]{0,1:T(8,128)(2,1)}, bf16[96,768]{1,0:T(8,128)(2,1)}, bf16[96,768]{1,0:T(8,1...) async-done(((bf16[96,2304]{0,1:T(8,128)(2,1)}, bf16[96,1536]{0,1:T(8,128)(2,1)}, bf16[96,768]{1,0:T(8,128)(2,1)}, ...) | async-done | bytes 2359312 | tf_op jit(solution)/shard_map/psum | solution.py:403
  (307 shorter events, 176.2 us)
Async XLA Ops:
  7.2 340.0 %reduce-scatter.20.cloned.1.call-start = ((), (), s32[]{:S(2)}) async-start(), calls=%async_computation.11 | async-start | bytes 2654208 | tf_op jit(solution)/shard_map/reduce_scatter | solution.py:382
  25.4 170.0 %copy-start.42 = (f32[256]{0:T(256)}, f32[256]{0:T(256)S(1)}, u32[]{:S(2)}) copy-start(f32[256]{0:T(256)S(1)} %broadcast_multiply_fusion.2) | copy-start | bytes 3076
  26.2 169.1 %copy-start.46 = (f32[256]{0:T(256)}, f32[256]{0:T(256)S(1)}, u32[]{:S(2)}) copy-start(f32[256]{0:T(256)S(1)} %fusion.74) | copy-start | bytes 3076
  149.8 5.1 copy-start.38
  195.4 13.5 %slice-start = ((s8[4718592]{0:T(1024)(128)(4,1)}), s8[4194304]{0:T(1024)(128)(4,1)S(1)}, s32[]{:S(2)}) async-start(s8[4718592]{0:T(1024)(128)(4,1)} %bitcast.204), calls=%async_computation.20 | async-start | bytes 8388608
  197.9 20.8 %copy-start.7 = (f32[256,768]{1,0:T(8,128)}, f32[256,768]{1,0:T(8,128)S(1)}, u32[]{:S(2)}) copy-start(f32[256,768]{1,0:T(8,128)S(1)} %get-tuple-element.234) | copy-start | bytes 2359300
  197.9 20.8 %copy-start.48 = (f32[256]{0:T(256)}, f32[256]{0:T(256)S(1)}, u32[]{:S(2)}) copy-start(f32[256]{0:T(256)S(1)} %broadcast_multiply_fusion.1) | copy-start | bytes 3076
  198.1 20.5 %copy-start.52 = (f32[256]{0:T(256)}, f32[256]{0:T(256)S(1)}, u32[]{:S(2)}) copy-start(f32[256]{0:T(256)S(1)} %fusion.75) | copy-start | bytes 3076
  199.0 9.9 slice-start.1
  199.0 9.9 copy-start.65
  228.2 4.9 copy-start.47
  235.2 145.8 %reduce-scatter.18.cloned.1.call-start = ((), (), s32[]{:S(2)}) async-start(), calls=%async_computation.10 | async-start | bytes 2654208 | tf_op jit(solution)/shard_map/reduce_scatter | solution.py:381
  235.2 7.5 copy-start.28
  244.6 207.9 %reduce-scatter.22.cloned.1.call-start = ((), (), s32[]{:S(2)}) async-start(), calls=%async_computation.12 | async-start | bytes 2654208 | tf_op jit(solution)/shard_map/reduce_scatter | solution.py:377
  247.8 302.7 %reduce-scatter.32.cloned.1.call-start = ((), (), s32[]{:S(2)}) async-start(), calls=%async_computation.17 | async-start | bytes 5308416
  288.9 393.9 %reduce-scatter.28.cloned.1.call-start = ((), (), s32[]{:S(2)}) async-start(), calls=%async_computation.15 | async-start | bytes 7962624
  313.6 535.7 %reduce-scatter.24.cloned.1.call-start = ((), (), s32[]{:S(2)}) async-start(), calls=%async_computation.13 | async-start | bytes 10616832 | tf_op jit(solution)/shard_map/reduce_scatter | solution.py:375
  321.1 694.8 %reduce-scatter.26.cloned.1.call-start = ((), (), s32[]{:S(2)}) async-start(), calls=%async_computation.14 | async-start | bytes 10616832 | tf_op jit(solution)/shard_map/reduce_scatter | solution.py:376
  327.9 13.3 %copy-start.45 = (f32[12,64]{1,0:T(8,128)S(1)}, f32[12,64]{1,0:T(8,128)}, u32[]{:S(2)}) copy-start(f32[12,64]{1,0:T(8,128)} %get-tuple-element.244) | copy-start | bytes 9220
  328.0 752.2 %reduce-scatter.34.cloned.1.call-start = ((), (), s32[]{:S(2)}) async-start(), calls=%async_computation.18 | async-start | bytes 442368
  335.0 809.2 %reduce-scatter.30.cloned.1.call-start = ((), (), s32[]{:S(2)}) async-start(), calls=%async_computation.16 | async-start | bytes 442368
  347.1 861.7 %all-reduce.11.cloned.1.call-start = ((), (), s32[]{:S(2)}) async-start(), calls=%async_computation.19 | async-start | bytes 5210112 | tf_op jit(solution)/shard_map/psum | solution.py:403
  685.1 333.0 %copy-start.62 = (f32[256]{0:T(256)S(1)}, f32[256]{0:T(256)}, u32[]{:S(2)}) copy-start(f32[256]{0:T(256)} %copy-done.61) | copy-start | bytes 3076
  1018.1 5.4 copy-start.54
  (56 other events, 110.3 us)
Sparse Core Ops, SparseCore 0:
  235.3 73.8 reduce-scatter.19
  312.7 68.2 reduce-scatter.17
  384.4 68.0 reduce-scatter.21
  456.0 94.4 reduce-scatter.31
  554.1 128.7 reduce-scatter.27
  686.8 162.5 reduce-scatter.23
  853.3 162.5 reduce-scatter.25
  1019.5 60.5 reduce-scatter.33
  1083.7 60.4 reduce-scatter.29
  1148.9 59.9 all-reduce.10
where the time goes:
time: 1240 us; the launch traced here: 1230 us
  waiting for transfers between devices  789 us (64%)
  local copies, waits for them, and re-layouts  157 us (13%)
  blocking collectives  124 us (10%)
  matrix products  90.2 us (7%)
  other arithmetic  51.1 us (4%)
  between operations  16.9 us (1%)
    unnamed x14, waiting for transfers between devices  306 us
    reduce_scatter x1, waiting for transfers between devices, on_device(): lax.psum_scatter(d_ffn_out, 'blk', scatter_dimension=0, tiled=True)  164 us
    reduce_scatter x1, waiting for transfers between devices, on_device(): lax.psum_scatter(d_ffn_in, 'blk', scatter_dimension=0, tiled=True)  164 us
    unnamed x155, local copies, waits for them, and re-layouts  112 us
    reduce_scatter x1, waiting for transfers between devices, on_device(): lax.psum_scatter(d_cross_out, 'blk', scatter_dimension=0, tiled=True)  69.9 us
    psum x1, waiting for transfers between devices, on_device(): lax.psum(g_self_qkv.astype(jnp.bfloat16), 'rep').astype(jnp.float32)  52.2 us
    unnamed x1, blocking collectives  35.2 us
    all_gather x1, blocking collectives, on_device(): lax.all_gather(store_keys, 'blk', axis=0, tiled=True)  34.4 us
  transfers between devices with their start and end apart: 10, of which 9 were waited for; matrix products, arithmetic and copies ran while one was open for 10% of the time, Pallas kernels for 0%

commit v1 on v0

v1 whole, which is shorter than its diff:
```python
import functools

import jax
import jax.numpy as jnp
from jax import lax
from jax.experimental import pallas as pl
from jax.experimental.pallas import tpu as pltpu
from jax.sharding import PartitionSpec as P

D = 768
HEADS = 12
HD = 64
FF = 3072
EPS = 1e-05
NEG = -1e30
BF = jnp.bfloat16
F32 = jnp.float32
MESH = pl.DeviceIdType.MESH
VMEM_LIMIT = 62 * 2**20

C_INNER, C_PROJ, C_SB, C_CQ, C_CB, C_FB, C_ALL = 0, 3072, 5376, 6144, 6912, 7680, 8448
R_SECOND, R_TOK, R_SMIX, R_FIRST, R_CMIX, R_ALL = 0, 768, 1536, 2304, 3072, 3840
N_VEC = 17


def dot(a, b):
    return lax.dot_general(a, b, (((1,), (0,)), ((), ())), preferred_element_type=F32)


def dot_nt(a, b):
    return lax.dot_general(a, b, (((1,), (1,)), ((), ())), preferred_element_type=F32)


def dot_tn(a, b):
    return lax.dot_general(a, b, (((0,), (0,)), ((), ())), preferred_element_type=F32)


def at(index, size):
    return pl.ds(pl.multiple_of(index * size, size), size)


def half_mask(half):
    lane = lax.broadcasted_iota(jnp.int32, (1, 2 * HD), 1)
    return ((lane >= HD) if half else (lane < HD)).astype(F32).astype(BF)


def partial_rows(values):
    rows, width = values.shape
    return jnp.sum(values.reshape(rows // 8, 8, width), axis=0)


def total_row(values):
    return jnp.sum(values, axis=0, keepdims=True)


def gelu_and_slope(v):
    cdf = 0.5 * (1.0 + lax.erf(v * 0.7071067811865476))
    return v * cdf, cdf + v * (jnp.exp(-0.5 * v * v) * 0.3989422804014327)


def norm_rows(r):
    centered = r - jnp.mean(r, axis=-1, keepdims=True)
    rstd = lax.rsqrt(jnp.mean(centered * centered, axis=-1, keepdims=True) + EPS)
    return centered * rstd, rstd


def norm_rows_back(grad, xhat, rstd, gain):
    e = grad * gain
    mean_e = jnp.mean(e, axis=-1, keepdims=True)
    mean_x = jnp.mean(e * xhat, axis=-1, keepdims=True)
    return (e - mean_e - xhat * mean_x) * rstd


def row_blocks(rows, block, body, init):
    return lax.fori_loop(0, rows // block, lambda i, c: body(at(i, block), i, c), init)


def attend(q_ref, k_ref, vt_ref, bias_ref, p_ref, mix_t_ref):
    def pair(j, _):
        cols = at(j, 2 * HD)
        q2, k2 = q_ref[:, cols], k_ref[:, cols]
        for half in range(2):
            h = 2 * j + half
            st = dot_nt(k2 * half_mask(half), q2) + bias_ref[...]
            e = jnp.exp(st - jnp.max(st, axis=0, keepdims=True))
            p = (e * (1.0 / jnp.sum(e, axis=0, keepdims=True))).astype(BF)
            p_ref[h] = p
            rows = at(h, HD)
            mix_t_ref[rows, :] = dot(vt_ref[rows, :], p).astype(BF)
        return 0

    lax.fori_loop(0, HEADS // 2, pair, 0)


def attend_back(p_ref, dmix_ref, q_ref, v_ref, kt_ref, dq_t_ref, put):
    def pair(j, _):
        cols = at(j, 2 * HD)
        dm2, q2, v2 = dmix_ref[:, cols], q_ref[:, cols], v_ref[:, cols]
        dk = dv = None
        for half in range(2):
            h = 2 * j + half
            mask = half_mask(half)
            dp = dot_nt(v2 * mask, dm2)
            pb = p_ref[h]
            p = pb.astype(F32)
            t = p * dp
            ds = (t - p * jnp.sum(t, axis=0, keepdims=True)).astype(BF)
            rows = at(h, HD)
            dq_t_ref[rows, :] = dot(kt_ref[rows, :], ds).astype(BF)
            dk_h, dv_h = dot(ds, q2 * mask), dot(pb, dm2 * mask)
            dk = dk_h if dk is None else dk + dk_h
            dv = dv_h if dv is None else dv + dv_h
        put(j, dk, dv)
        return 0

    lax.fori_loop(0, HEADS // 2, pair, 0)


def layer_kernel(
    tokens, states, retrieved, live, lengths, self_bias, self_out_bias, norm1, cq_bias, cv_bias, co_bias, norm2,
    fi_bias, fo_bias, norm3, cotangent, w_qkv_h, w_so_h, w_cq_h, w_ckv_h, w_co_h, w_fi_h, w_fo_h,
    result, d_hidden, xt, act_t, dmat, dkv, dstore, vec,
    w_qkv, w_so, w_cq, w_ckv, w_co, w_fi, w_fo, w_sem,
    q, k, v, vt, bias_s, p_s, sk, sv, svt, bias_c, p_c, cquery, mix_b, dmix,
    acc, acc2, first, xhat1, xhat2, second, sec_b, act, slope, d_res, dqt, rstd1, rstd2,
):
    rows = tokens.shape[0]
    slots = states.shape[0]
    length = lengths[0, 0]
    scale = HD**-0.5
    copies = []
    for i, (src, dst) in enumerate(
        [(w_qkv_h, w_qkv), (w_so_h, w_so), (w_cq_h, w_cq), (w_ckv_h, w_ckv), (w_co_h, w_co), (w_fi_h, w_fi), (w_fo_h, w_fo)]
    ):
        copies.append(pltpu.make_async_copy(src, dst, w_sem.at[i]))
        copies[-1].start()

    key_at = lax.broadcasted_iota(jnp.int32, (rows, rows), 0)
    query_at = lax.broadcasted_iota(jnp.int32, (rows, rows), 1)
    bias_s[...] = jnp.where((key_at <= query_at) & (key_at < length), 0.0, NEG)
    topk = retrieved.shape[1]
    slot_rank = lax.broadcasted_iota(jnp.int32, (rows, topk), 1)
    chosen = jnp.where((live[...] > 0) | (slot_rank == 0), retrieved[...], -1).T

    def mask_rows(i, _):
        ids = lax.broadcasted_iota(jnp.int32, (32, rows), 0) + i * 32
        hit = jnp.zeros((32, rows), jnp.bool_)
        for j in range(topk):
            hit = hit | (ids == chosen[j : j + 1, :])
        bias_c[at(i, 32), :] = jnp.where(hit, 0.0, NEG)
        return 0

    lax.fori_loop(0, slots // 32, mask_rows, 0)

    xt[R_TOK : R_TOK + D, :] = tokens[...].T
    copies[0].wait()
    q[...] = (dot(tokens[...], w_qkv[:, :D]) + self_bias[0:1, :]).astype(BF) * scale
    k[...] = dot(tokens[...], w_qkv[:, D : 2 * D]).astype(BF)
    v[...] = (dot(tokens[...], w_qkv[:, 2 * D :]) + self_bias[1:2, :]).astype(BF)
    vt[...] = v[...].T
    attend(q, k, vt, bias_s, p_s, xt.at[R_SMIX : R_SMIX + D])
    vt[...] = k[...].T * scale
    copies[1].wait()
    mix_b[...] = xt[R_SMIX : R_SMIX + D, :].T
    acc[...] = dot(mix_b[...], w_so[...])

    def ln1(rs, i, c):
        xhat, rstd = norm_rows(tokens[rs, :].astype(F32) + acc[rs, :] + self_out_bias[...][None, :])
        f = xhat * norm1[0:1, :] + norm1[1:2, :]
        xhat1[rs, :] = xhat
        rstd1[rs, :] = rstd
        first[rs, :] = f
        sec_b[rs, :] = f.astype(BF)
        return c

    row_blocks(rows, 32, ln1, 0)
    xt[R_FIRST : R_FIRST + D, :] = sec_b[...].T

    copies[2].wait()
    cquery[...] = (dot(sec_b[...], w_cq[...]) + cq_bias[...][None, :]).astype(BF) * scale
    copies[3].wait()
    sk[...] = dot(states[...], w_ckv[:, :D]).astype(BF)
    sv[...] = (dot(states[...], w_ckv[:, D:]) + cv_bias[...][None, :]).astype(BF)
    svt[...] = sv[...].T
    attend(cquery, sk, svt, bias_c, p_c, xt.at[R_CMIX : R_CMIX + D])
    svt[...] = sk[...].T * scale
    copies[4].wait()
    mix_b[...] = xt[R_CMIX : R_CMIX + D, :].T
    acc[...] = dot(mix_b[...], w_co[...])

    def ln2(rs, i, c):
        xhat, rstd = norm_rows(first[rs, :] + acc[rs, :] + co_bias[...][None, :])
        s = xhat * norm2[0:1, :] + norm2[1:2, :]
        xhat2[rs, :] = xhat
        rstd2[rs, :] = rstd
        second[rs, :] = s
        sec_b[rs, :] = s.astype(BF)
        return c

    row_blocks(rows, 32, ln2, 0)
    xt[R_SECOND : R_SECOND + D, :] = sec_b[...].T

    copies[5].wait()
    copies[6].wait()
    acc[...] = jnp.zeros_like(acc)

    def ffn(j, _):
        cols = at(j, D)
        acc2[...] = dot(sec_b[...], w_fi[:, cols])
        bias = fi_bias[pl.ds(j, 1), :]

        def gelu(rs, i, c):
            a, s = gelu_and_slope(acc2[rs, :] + bias)
            act[rs, :] = a.astype(BF)
            slope[rs, cols] = s.astype(BF)
            return c

        row_blocks(rows, 16, gelu, 0)
        act_t[cols, :] = act[...].T
        acc[...] += dot(act[...], w_fo[cols, :])
        return 0

    lax.fori_loop(0, FF // D, ffn, 0)
    zero = jnp.zeros((8, D), F32)

    def ln3(rs, i, c):
        xhat, rstd = norm_rows(second[rs, :] + acc[rs, :] + fo_bias[...][None, :])
        result[rs, :] = (xhat * norm3[0:1, :] + norm3[1:2, :]).astype(BF)
        place = lax.broadcasted_iota(jnp.int32, (32, 1), 0) + i * 32
        g = cotangent[rs, :].astype(F32) * jnp.where(place < length, 1.0, 0.0)
        d = norm_rows_back(g, xhat, rstd, norm3[0:1, :])
        d_res[rs, :] = d
        db = d.astype(BF)
        dmat[rs, C_FB : C_FB + D] = db
        return (c[0] + partial_rows(g * xhat), c[1] + partial_rows(g), c[2] + partial_rows(db.astype(F32)))

    sums = row_blocks(rows, 32, ln3, (zero, zero, zero))
    vec[N_VEC:, :] = jnp.zeros((vec.shape[0] - N_VEC, D), F32)
    vec[11:12, :], vec[12:13, :], vec[10:11, :] = (total_row(s) for s in sums)

    acc[...] = d_res[...]

    def ffn_back(j, _):
        cols = at(j, D)
        acc2[...] = dot_nt(dmat[:, C_FB : C_FB + D], w_fo[cols, :])

        def inner(rs, i, c):
            d = (slope[rs, cols].astype(F32) * acc2[rs, :]).astype(BF)
            act[rs, :] = d
            return c + partial_rows(d.astype(F32))

        vec[pl.ds(13 + j, 1), :] = total_row(row_blocks(rows, 32, inner, zero))
        dmat[:, cols] = act[...]
        acc[...] += dot_nt(act[...], w_fi[:, cols])
        return 0

    lax.fori_loop(0, FF // D, ffn_back, 0)

    def ln2_back(rs, i, c):
        g, xhat = acc[rs, :], xhat2[rs, :]
        d = norm_rows_back(g, xhat, rstd2[rs, :], norm2[0:1, :])
        d_res[rs, :] = d
        db = d.astype(BF)
        dmat[rs, C_CB : C_CB + D] = db
        return (c[0] + partial_rows(g * xhat), c[1] + partial_rows(g), c[2] + partial_rows(db.astype(F32)))

    sums = row_blocks(rows, 32, ln2_back, (zero, zero, zero))
    vec[8:9, :], vec[9:10, :], vec[7:8, :] = (total_row(s) for s in sums)

    dmix[...] = dot_nt(dmat[:, C_CB : C_CB + D], w_co[...]).astype(BF)

    def put_store(j, dk, dv):
        dkv[:, at(j, 2 * HD)] = dk.astype(BF)
        dkv[:, pl.ds(pl.multiple_of(D + j * 2 * HD, 2 * HD), 2 * HD)] = dv.astype(BF)
        vec[pl.ds(6, 1), at(j, 2 * HD)] = total_row(dv)

    attend_back(p_c, dmix, cquery, sv, svt, dqt, put_store)
    dstore[...] = dot_nt(dkv[...], w_ckv[...]).astype(BF)
    dq = dqt[...].T
    dmat[:, C_CQ : C_CQ + D] = dq
    vec[5:6, :] = total_row(partial_rows(dq.astype(F32)))
    acc[...] = d_res[...] + dot_nt(dq, w_cq[...])

    def ln1_back(rs, i, c):
        g, xhat = acc[rs, :], xhat1[rs, :]
        d = norm_rows_back(g, xhat, rstd1[rs, :], norm1[0:1, :])
        d_res[rs, :] = d
        db = d.astype(BF)
        dmat[rs, C_SB : C_SB + D] = db
        return (c[0] + partial_rows(g * xhat), c[1] + partial_rows(g), c[2] + partial_rows(db.astype(F32)))

    sums = row_blocks(rows, 32, ln1_back, (zero, zero, zero))
    vec[3:4, :], vec[4:5, :], vec[2:3, :] = (total_row(s) for s in sums)

    dmix[...] = dot_nt(dmat[:, C_SB : C_SB + D], w_so[...]).astype(BF)

    def put_self(j, dk, dv):
        dvb = dv.astype(BF)
        dmat[:, pl.ds(pl.multiple_of(C_PROJ + D + j * 2 * HD, 2 * HD), 2 * HD)] = dk.astype(BF)
        dmat[:, pl.ds(pl.multiple_of(C_PROJ + 2 * D + j * 2 * HD, 2 * HD), 2 * HD)] = dvb
        vec[pl.ds(1, 1), at(j, 2 * HD)] = total_row(dvb.astype(F32))

    attend_back(p_s, dmix, q, v, vt, dqt, put_self)
    dq = dqt[...].T
    dmat[:, C_PROJ : C_PROJ + D] = dq
    vec[0:1, :] = total_row(partial_rows(dq.astype(F32)))
    d_hidden[...] = d_res[...] + dot_nt(dmat[:, C_PROJ : C_PROJ + 3 * D], w_qkv[...])


def run_layer(args, states_all):
    (hidden, store, retrieved, live, lengths, self_qkv, self_bias, self_out, self_out_bias, norm1, cross_q, cross_q_bias,
     cross_kv, cross_v_bias, cross_out, cross_out_bias, norm2, ffn_in, ffn_in_bias, ffn_out, ffn_out_bias, norm3, cotangent) = args
    rows, slots = hidden.shape[2], states_all.shape[0]
    shape = jax.ShapeDtypeStruct
    vmem, hbm, smem = (pl.BlockSpec(memory_space=m) for m in (pltpu.VMEM, pl.ANY, pltpu.SMEM))
    weights = (self_qkv, self_out, cross_q, cross_kv, cross_out, ffn_in, ffn_out)
    scratch = [pltpu.VMEM(w.shape, BF) for w in weights] + [pltpu.SemaphoreType.DMA((len(weights),))]
    wide = (rows, D)
    for dims, kind in [
        (wide, BF), (wide, BF), (wide, BF), ((D, rows), BF), ((rows, rows), F32), ((HEADS, rows, rows), BF),
        ((slots, D), BF), ((slots, D), BF), ((D, slots), BF), ((slots, rows), F32), ((HEADS, slots, rows), BF),
        (wide, BF), (wide, BF), (wide, BF), (wide, F32), (wide, F32), (wide, F32), (wide, F32), (wide, F32), (wide, F32),
        (wide, BF), (wide, BF), ((rows, FF), BF), (wide, F32), ((D, rows), BF), ((rows, 1), F32), ((rows, 1), F32),
    ]:
        scratch.append(pltpu.VMEM(dims, kind))
    return pl.pallas_call(
        layer_kernel,
        out_shape=(
            shape(wide, BF), shape(wide, F32), shape((R_ALL, rows), BF), shape((FF, rows), BF),
            shape((rows, C_ALL), BF), shape((slots, 2 * D), BF), shape((slots, D), BF), shape((24, D), F32),
        ),
        in_specs=[vmem] * 4 + [smem] + [vmem] * 11 + [hbm] * 7,
        out_specs=(vmem,) * 8,
        scratch_shapes=scratch,
        compiler_params=pltpu.CompilerParams(vmem_limit_bytes=VMEM_LIMIT),
        cost_estimate=pl.CostEstimate(flops=10**10, bytes_accessed=5 * 10**7, transcendentals=10**6),
    )(
        hidden[0, 0], states_all, retrieved[0, 0], live[0, 0], lengths, self_bias, self_out_bias, norm1, cross_q_bias,
        cross_v_bias, cross_out_bias, norm2, ffn_in_bias.reshape(FF // D, D), ffn_out_bias, norm3, cotangent[0, 0], *weights,
    )


def gather_kernel(n, states, whole, held, send_sem, recv_sem):
    me, rep = lax.axis_index("blk"), lax.axis_index("rep")
    barrier = pltpu.get_barrier_semaphore()
    for step in range(1, n):
        pl.semaphore_signal(barrier, inc=1, device_id=(lax.rem(me + step, n), rep), device_id_type=MESH)
    held[me] = states[...]
    pl.semaphore_wait(barrier, n - 1)
    copies = []
    for step in range(1, n):
        copies.append(
            pltpu.make_async_remote_copy(
                src_ref=states, dst_ref=held.at[me], send_sem=send_sem.at[step - 1], recv_sem=recv_sem.at[step - 1],
                device_id=(lax.rem(me + step, n), rep), device_id_type=MESH,
            )
        )
        copies[-1].start()
    for copy in copies:
        copy.wait()
    whole[...] = held[...]


def gather_states(states, n):
    block = states.shape
    vmem = pl.BlockSpec(memory_space=pltpu.VMEM)
    whole = pl.pallas_call(
        functools.partial(gather_kernel, n),
        out_shape=jax.ShapeDtypeStruct((n, *block), BF),
        in_specs=[vmem],
        out_specs=vmem,
        scratch_shapes=[pltpu.VMEM((n, *block), BF), pltpu.SemaphoreType.DMA((n - 1,)), pltpu.SemaphoreType.DMA((n - 1,))],
        compiler_params=pltpu.CompilerParams(collective_id=0, has_side_effects=True),
    )(states)
    return whole.reshape(n * block[0], block[1])


PART = 384
SHARD = D // 8
PAIRS = 8
PIECES = [("fo", i) for i in range(4)] + [("fi", i) for i in range(4)]
PIECES += [("co", 0), ("cq", 0), ("ckv", 0), ("ckv", 1), ("so", 0), ("qkv", 0), ("qkv", 1), ("qkv", 2)]
H_INNER, H_PROJ, H_SB, H_CQ, H_CB, H_FB, H_ALL = 0, 1536, 2688, 3072, 3456, 3840, 4608


def sum_kernel(
    xt, act_t, states, dmat, dkv, dstore, vec, fin_out, dstore_out, vec_out,
    xc, ac, sc, dc, dkc, l_sem, os_sem, or_sem,
    g, ax, hx, az, hz, ay, by, hy, bx, hbx, bz, fin,
    axs, axr, azs, azr, ays, ayr, bys, byr, bxs, bxr, bzs, bzr, bgs, bgr, cs, cr, f_sem,
    ds_in, vsh, vin, vrep, dss, dsr, vss, vsr, vps, vpr, v_sem,
):
    b, r = lax.axis_index("blk"), lax.axis_index("rep")
    z, x, y, c = b // 2, b % 2, r // 2, r % 2
    rows = dmat.shape[0]
    slots = states.shape[0]
    at_x = (z * 2 + 1 - x, r)
    at_y = (b, (1 - y) * 2 + c)
    at_c = (b, y * 2 + 1 - c)
    at_z = [(lax.rem(z + step, 4) * 2 + x, r) for step in range(1, 4)]
    at_blk = [(lax.rem(b + step, 8), r) for step in range(1, 8)]
    at_rep = [(b, lax.rem(r + step, 4)) for step in range(1, 4)]

    def send(src, dst, s_sem, r_sem, device):
        copy = pltpu.make_async_remote_copy(
            src_ref=src, dst_ref=dst, send_sem=s_sem, recv_sem=r_sem, device_id=device, device_id_type=MESH
        )
        copy.start()
        return copy

    barrier = pltpu.get_barrier_semaphore()
    for device in at_blk + at_rep:
        pl.semaphore_signal(barrier, inc=1, device_id=device, device_id_type=MESH)

    def halves(who):
        def cols(start, width):
            return pl.ds(pl.multiple_of(start + who * width, 128), width)

        return [
            (act_t.at[:, who], ac.at[:, :, 0:rows], ac.at[:, :, rows:]),
            (dmat.at[:, C_FB : C_FB + D], dc.at[0:rows, H_FB : H_FB + D], dc.at[rows:, H_FB : H_FB + D]),
            (xt.at[0:D], xc.at[0:D, 0:rows], xc.at[0:D, rows:]),
            (dmat.at[:, cols(C_INNER, 1536)], dc.at[0:rows, 0:1536], dc.at[rows:, 0:1536]),
            (xt.at[D:R_ALL], xc.at[D:R_ALL, 0:rows], xc.at[D:R_ALL, rows:]),
            (dmat.at[:, cols(C_PROJ, 1152)], dc.at[0:rows, H_PROJ:H_SB], dc.at[rows:, H_PROJ:H_SB]),
            (dmat.at[:, cols(C_SB, 384)], dc.at[0:rows, H_SB:H_CQ], dc.at[rows:, H_SB:H_CQ]),
            (dmat.at[:, cols(C_CQ, 384)], dc.at[0:rows, H_CQ:H_CB], dc.at[rows:, H_CQ:H_CB]),
            (dmat.at[:, cols(C_CB, 384)], dc.at[0:rows, H_CB:H_FB], dc.at[rows:, H_CB:H_FB]),
            (states, sc.at[0:slots], sc.at[slots:]),
            (dkv.at[:, cols(0, D)], dkc.at[0:slots], dkc.at[slots:]),
        ]

    mine, theirs = halves(c), halves(1 - c)
    local = []
    for i, (src, dst, _) in enumerate(mine):
        local.append(pltpu.make_async_copy(src, dst, l_sem.at[i]))
        local[-1].start()
    vsh[...] = jnp.zeros_like(vsh)
    for s in range(8):
        vsh[s, 0:13, 0:SHARD] = vec[0:13, s * SHARD : (s + 1) * SHARD]
        for part in range(4):
            begin = 384 * s + SHARD * part
            vsh[s, 13 + part : 14 + part, 0:SHARD] = vec[13 + begin // D : 14 + begin // D, begin % D : begin % D + SHARD]
    pl.semaphore_wait(barrier, len(at_blk) + len(at_rep))
    sent = []
    exchange = []
    for i, (src, _, dst) in enumerate(theirs):
        exchange.append(send(src, dst, os_sem.at[i], or_sem.at[i], at_c))
    sent += exchange
    small_d, small_v = [], []
    for i, device in enumerate(at_blk):
        small_d.append(send(dstore.at[device[0]], ds_in.at[i], dss.at[i], dsr.at[i], device))
        small_v.append(send(vsh.at[device[0]], vin.at[i], vss.at[i], vsr.at[i], device))
    sent += small_d + small_v

    arrived = [False] * len(mine)

    def need(*which):
        for i in which:
            if not arrived[i]:
                local[i].wait()
                exchange[i].wait_recv()
                arrived[i] = True

    def product(i):
        kind, part = PIECES[i]
        if kind == "fo":
            need(0, 1)
            left = ac[:, (part // 2) * SHARD : (part // 2 + 1) * SHARD, :].reshape(8 * SHARD, 2 * rows)
            right = dc[:, H_FB + (part % 2) * PART : H_FB + (part % 2 + 1) * PART]
        elif kind == "ckv":
            need(9, 10)
            left, right = sc[...].T, dkc[:, part * PART : (part + 1) * PART]
        else:
            uses, row, col = {
                "fi": ((2, 3), R_SECOND, H_INNER), "co": ((4, 8), R_CMIX, H_CB), "cq": ((4, 7), R_FIRST, H_CQ),
                "so": ((4, 6), R_SMIX, H_SB), "qkv": ((4, 5), R_TOK, H_PROJ),
            }[kind]
            need(*uses)
            left, right = xc[row : row + D, :], dc[:, col + part * PART : col + (part + 1) * PART]
        g[i] = dot(left, right).astype(BF).reshape(4, 2, 2, SHARD // 2, PART)

    steps_a = [[None] * PAIRS for _ in range(4)]
    steps_b = [[None] * PAIRS for _ in range(5)]

    def a0(t):
        product(2 * t)
        steps_a[0][t] = send(g.at[2 * t, :, 1 - x], ax.at[t], axs.at[t], axr.at[t], at_x)

    def a1(t):
        steps_a[0][t].wait_recv()
        hx[t] = g[2 * t, :, x] + ax[t]
        steps_a[1][t] = []
        for i, device in enumerate(at_z):
            steps_a[1][t].append(send(hx.at[t, device[0] // 2], az.at[t, i], azs.at[t, i], azr.at[t, i], device))

    def a2(t):
        for copy in steps_a[1][t]:
            copy.wait_recv()
        own, far = hx[t, z], az[t]
        hz[t] = ((own.astype(F32) + far[0].astype(F32)) + (far[1].astype(F32) + far[2].astype(F32))).astype(BF)
        steps_a[2][t] = send(hz.at[t], ay.at[t], ays.at[t], ayr.at[t], at_y)

    def finish(i):
        steps = steps_a[3] if i % 2 == 0 else steps_b[4]
        steps[i // 2] = send(fin.at[i, c], fin.at[i, c], cs.at[i], cr.at[i], at_c)

    def a3(t):
        steps_a[2][t].wait_recv()
        fin[2 * t, c] = hz[t] + ay[t]
        finish(2 * t)

    def b0(t):
        product(2 * t + 1)
        steps_b[0][t] = send(g.at[2 * t + 1, :, :, 1 - y], by.at[t], bys.at[t], byr.at[t], at_y)

    def b1(t):
        steps_b[0][t].wait_recv()
        hy[t] = g[2 * t + 1, :, :, y] + by[t]
        steps_b[1][t] = send(hy.at[t, :, 1 - x], bx.at[t], bxs.at[t], bxr.at[t], at_x)

    def b2(t):
        steps_b[1][t].wait_recv()
        hbx[t] = hy[t, :, x] + bx[t]
        steps_b[2][t] = []
        for i, device in enumerate(at_z):
            steps_b[2][t].append(send(hbx.at[t, device[0] // 2], bz.at[t, i], bzs.at[t, i], bzr.at[t, i], device))

    def b3(t):
        for copy in steps_b[2][t]:
            copy.wait_recv()
        own, far = hbx[t, z], bz[t]
        total = (own.astype(F32) + far[0].astype(F32)) + (far[1].astype(F32) + far[2].astype(F32))
        fin[2 * t + 1, c, y] = total.astype(BF)
        steps_b[3][t] = send(fin.at[2 * t + 1, c, y], fin.at[2 * t + 1, c, y], bgs.at[t], bgr.at[t], at_y)

    def b4(t):
        steps_b[3][t].wait_recv()
        finish(2 * t + 1)

    out = []

    def close(i):
        (steps_a[3] if i % 2 == 0 else steps_b[4])[i // 2].wait_recv()
        out.append(pltpu.make_async_copy(fin.at[i], fin_out.at[i], f_sem.at[i]))
        out[-1].start()

    small = []
    for tick in range(PAIRS + 6):
        for body, lag in (
            (a0, 0), (b0, 0), (a1, 1), (b1, 1), (a2, 2), (b2, 2), (a3, 3), (b3, 3), (b4, 4),
            (lambda t: close(2 * t), 4), (lambda t: close(2 * t + 1), 5),
        ):
            if 0 <= tick - lag < PAIRS:
                body(tick - lag)
        if tick == 2:
            total = dstore[b].astype(F32)
            for i, copy in enumerate(small_d):
                copy.wait_recv()
                total = total + ds_in[i].astype(F32)
            dstore_out[...] = total
            total = vsh[b]
            for i, copy in enumerate(small_v):
                copy.wait_recv()
                total = total + vin[i]
            vrep[r] = total
            for i, device in enumerate(at_rep):
                small.append(send(vrep.at[r], vrep.at[r], vps.at[i], vpr.at[i], device))
            sent += small
        if tick == 4:
            for copy in small:
                copy.wait_recv()
            vec_out[...] = (vrep[0] + vrep[1]) + (vrep[2] + vrep[3])
    for steps in steps_a + steps_b:
        for entry in steps:
            sent += entry if isinstance(entry, list) else [entry]
    for copy in sent:
        copy.wait_send()
    for copy in out:
        copy.wait()


def sum_gradients(states, xt, act_t, dmat, dkv, dstore, vec):
    rows, slots = dmat.shape[0], states.shape[0]
    n = len(PIECES)
    vmem, hbm = (pl.BlockSpec(memory_space=m) for m in (pltpu.VMEM, pl.ANY))
    shape = jax.ShapeDtypeStruct
    sem = lambda *dims: pltpu.SemaphoreType.DMA(dims)
    buf = lambda *dims: pltpu.VMEM(dims, BF)
    p = PAIRS
    half = SHARD // 2
    scratch = [
        buf(R_ALL, 2 * rows), buf(8, 2 * SHARD, 2 * rows), buf(2 * slots, D), buf(2 * rows, H_ALL), buf(2 * slots, D),
        sem(11), sem(11), sem(11),
        buf(n, 4, 2, 2, half, PART), buf(p, 4, 2, half, PART), buf(p, 4, 2, half, PART), buf(p, 3, 2, half, PART),
        buf(p, 2, half, PART), buf(p, 2, half, PART), buf(p, 4, 2, half, PART), buf(p, 4, 2, half, PART),
        buf(p, 4, half, PART), buf(p, 4, half, PART), buf(p, 3, half, PART), buf(n, 2, 2, half, PART),
        sem(p), sem(p), sem(p, 3), sem(p, 3), sem(p), sem(p), sem(p), sem(p), sem(p), sem(p), sem(p, 3), sem(p, 3),
        sem(p), sem(p), sem(n), sem(n), sem(n),
        buf(7, slots // 8, D), pltpu.VMEM((8, 24, 128), F32), pltpu.VMEM((7, 24, 128), F32), pltpu.VMEM((4, 24, 128), F32),
        sem(7), sem(7), sem(7), sem(7), sem(3), sem(3), sem(1),
    ]
    return pl.pallas_call(
        sum_kernel,
        out_shape=(shape((n, 2, 2, half, PART), BF), shape((slots // 8, D), F32), shape((24, 128), F32)),
        in_specs=[hbm] * 5 + [vmem] * 2,
        out_specs=(hbm, vmem, vmem),
        scratch_shapes=scratch,
        compiler_params=pltpu.CompilerParams(collective_id=1, has_side_effects=True, vmem_limit_bytes=VMEM_LIMIT),
        cost_estimate=pl.CostEstimate(flops=5 * 10**9, bytes_accessed=3 * 10**7, transcendentals=0),
    )(xt, act_t.reshape(8, 2, 2 * SHARD, rows), states, dmat, dkv, dstore.reshape(8, slots // 8, D), vec)


def place_kernel(fin, dstore, vec, *outs):
    (o_dstore, o_qkv, o_sbias, o_so, o_sob, o_n1, o_cq, o_cqb, o_ckv, o_cvb, o_co, o_cob, o_n2, o_fi, o_fib, o_fo, o_fob, o_n3) = outs
    o_dstore[...] = dstore[...]
    wide = {"qkv": o_qkv, "so": o_so, "cq": o_cq, "ckv": o_ckv, "co": o_co, "fi": o_fi}
    for i, (kind, part) in enumerate(PIECES):
        for c in range(2):
            values = fin[i, c].astype(F32)
            if kind == "fo":
                begin = c * 2 * SHARD + (part // 2) * SHARD
                o_fo[begin : begin + SHARD, (part % 2) * PART : (part % 2 + 1) * PART] = values
            else:
                ref = wide[kind]
                begin = c * (ref.shape[1] // 2) + part * PART
                ref[:, begin : begin + PART] = values
    for ref, row in ((o_sbias, 0), (o_n1, 3), (o_n2, 8), (o_n3, 11)):
        ref[...] = vec[row : row + 2, 0:SHARD]
    for ref, row in ((o_sob, 2), (o_cqb, 5), (o_cvb, 6), (o_cob, 7), (o_fob, 10)):
        ref[...] = vec[row, 0:SHARD]
    for part in range(4):
        o_fib[pl.ds(part * SHARD, SHARD)] = vec[13 + part, 0:SHARD]


def place(fin, dstore, vec):
    shape = lambda *dims: jax.ShapeDtypeStruct(dims, F32)
    return pl.pallas_call(
        place_kernel,
        out_shape=(
            shape(*dstore.shape), shape(SHARD, 3 * D), shape(2, SHARD), shape(SHARD, D), shape(SHARD), shape(2, SHARD),
            shape(SHARD, D), shape(SHARD), shape(SHARD, 2 * D), shape(SHARD), shape(SHARD, D), shape(SHARD), shape(2, SHARD),
            shape(SHARD, FF), shape(FF // 8), shape(FF // 8, D), shape(SHARD), shape(2, SHARD),
        ),
        compiler_params=pltpu.CompilerParams(vmem_limit_bytes=VMEM_LIMIT),
    )(fin.reshape(len(PIECES), 2, SHARD, PART), dstore, vec)


def sum_plainly(states, xt, act_t, dmat, dkv, dstore, vec):
    def total(value, dim):
        part = lax.psum_scatter(value, "blk", scatter_dimension=dim, tiled=True)
        return lax.psum(part.astype(BF), "rep").astype(F32)

    def rows_of(start):
        return lax.slice_in_dim(xt, start, start + D, axis=0)

    def cols_of(start, width):
        return lax.slice_in_dim(dmat, start, start + width, axis=1)

    g_qkv = total(dot(rows_of(R_TOK), cols_of(C_PROJ, 3 * D)), 0)
    g_so = total(dot(rows_of(R_SMIX), cols_of(C_SB, D)), 0)
    g_cq = total(dot(rows_of(R_FIRST), cols_of(C_CQ, D)), 0)
    g_co = total(dot(rows_of(R_CMIX), cols_of(C_CB, D)), 0)
    g_fi = total(dot(rows_of(R_SECOND), cols_of(C_INNER, FF)), 0)
    g_fo = total(dot(act_t, cols_of(C_FB, D)), 0)
    g_ckv = total(dot_tn(states, dkv), 0)
    g_store = lax.psum_scatter(dstore.astype(F32), "blk", scatter_dimension=0, tiled=True)
    g_fib = total(vec[13:N_VEC].reshape(FF), 0)
    v = total(vec[:13].T, 0)
    two = lambda row: v[:, row : row + 2].T
    return (
        g_store, g_qkv, two(0), g_so, v[:, 2], two(3), g_cq, v[:, 5], g_ckv, v[:, 6], g_co, v[:, 7], two(8),
        g_fi, g_fib, g_fo, v[:, 10], two(11),
    )


def on_device(fast, n, *args):
    states = args[1][0]
    states_all = gather_states(states, n) if fast else lax.all_gather(states, "blk", axis=0, tiled=True)
    result, d_hidden, *operands = run_layer(args, states_all)
    if fast:
        grads = place(*sum_gradients(states_all, *operands))
    else:
        grads = sum_plainly(states_all, *operands)
    return (result[None, None], d_hidden[None, None], grads[0][None], *grads[1:])


def solution(mesh):
    n = mesh.shape["blk"]
    fast = n == 8 and mesh.shape["rep"] == 4
    deep, flat = P("rep", "blk", None, None), P("rep", "blk", None)
    in_specs = (deep, flat, deep, deep, P("rep", "blk")) + (P(),) * 17 + (deep,)
    w, vec, two = P("blk", None), P("blk"), P(None, "blk")
    out_specs = (deep, deep, flat, w, two, w, vec, two, w, vec, w, vec, w, vec, two, w, vec, w, vec, two)
    return jax.shard_map(
        functools.partial(on_device, fast, n), mesh=mesh, in_specs=in_specs, out_specs=out_specs, check_vma=False
    )
```

time: 1240 us -> 175 us (0.14)
  waiting for transfers between devices: 789 us -> 0 us
  Pallas kernels: 0 us -> 168 us
  local copies, waits for them, and re-layouts: 157 us -> 4.5 us
  blocking collectives: 124 us -> 0 us
  matrix products: 90.2 us -> 0 us
  other arithmetic: 51.1 us -> 0 us
  between operations: 16.9 us -> 1.49 us
    reduce_scatter x5 -> x0, waiting for transfers between devices: 431 us -> none  [the longest x1 164 us: on_device(): lax.psum_scatter(d_ffn_out, 'blk', scatter_dimension=0, tiled=True)]
    unnamed x14 -> x0, waiting for transfers between devices: 306 us -> none
    pallas_call x0 -> x4, Pallas kernels: none -> 168 us  [the longest x1 102 us: sum_gradients(): pl.pallas_call(sum_kernel, out_shape=(shape((n, 2, 2, half, PART), BF), s...]
    unnamed x155 -> x2, local copies, waits for them, and re-layouts: 112 us -> 3.19 us
    dot_general x33 -> x0, matrix products: 90.2 us -> none  [the longest x6 24.5 us: matmul_tn(): lax.dot_general(left_op, right_op, (((0,), (0,)), ((), ())), preferred_el...]
    all_gather x2 -> x0, blocking collectives: 67.4 us -> none  [the longest x1 34.4 us: on_device(): lax.all_gather(store_keys, 'blk', axis=0, tiled=True)]
    psum x1 -> x0, waiting for transfers between devices: 52.2 us -> none  [on_device(): lax.psum(g_self_qkv.astype(jnp.bfloat16), 'rep').astype(jnp.float32)]
    unnamed x1 -> x0, blocking collectives: 35.2 us -> none
  transfers between devices with their start and end apart: 10 -> 0, of which waited for: 9 -> 0; matrix products, arithmetic and copies ran while one was open for 10% -> 0% of each run, Pallas kernels for 0% -> 0%
where the time goes in v1:
time: 175 us; the launch traced here: 174 us
  Pallas kernels  168 us (96%)
  local copies, waits for them, and re-layouts  4.5 us (3%)
    pallas_call x1, Pallas kernels, sum_gradients(): pl.pallas_call(sum_kernel, out_shape=(shape((n, 2, 2, half, PART), BF), s...  102 us
    pallas_call x1, Pallas kernels, run_layer(): pl.pallas_call(layer_kernel, out_shape=(shape(wide, BF), shape(wide, F32)...  51.3 us
    pallas_call x1, Pallas kernels, gather_states(): pl.pallas_call(functools.partial(gather_kernel, n), out_shape=jax.ShapeDt...  11.2 us
    pallas_call x1, Pallas kernels, place(): pl.pallas_call(place_kernel, out_shape=(shape(*dstore.shape), shape(SHARD...  4 us

profile of v1, /device:TPU:0, one launch (start us, length us, event | category | flops | bytes accessed | tf_op | source)
XLA Modules:
  0.0 174.3 jit_solution(11280943867787045717)
XLA Ops:
  1.3 1.3 reshape.56.fi_bias
  2.6 1.6 copy.43
  4.2 1.6 copy.44
  5.8 11.2 %shard_map.374 = bf16[8,16,768]{2,1,0:T(8,128)(2,1)} custom-call(bf16[16,768]{1,0:T(8,128)(2,1)} %bitcast.17), custom_call_target="tpu_custom_call" | custom-call | tf_op jit(solution)/shard_map/pallas_call | solution.py:367
  17.1 51.3 %shard_map.375 = (bf16[256,768]{1,0:T(8,128)(2,1)}, f32[256,768]{1,0:T(8,128)}, bf16[3840,256]{1,0:T(8,128)(2,1)}, bf16[3072,256]{1,0:T(8,128)(2,1)}, bf16[256,8...) custom-call(bf16[256,768]{1,0:T(8,128)(2,1)} %bitcast.18, ...), custom_call_target="tpu_custom_call" | custom-call | flops 10000000000 | bytes 50000000 | tf_op jit(solution)/shard_map/pallas_call | solution.py:326
  68.3 101.8 %shard_map.376 = (bf16[16,2,2,48,384]{4,3,2,1,0:T(8,128)(2,1)}, f32[16,768]{1,0:T(8,128)}, f32[24,128]{1,0:T(8,128)}) custom-call(bf16[3840,256]{1,0:T(8,128)(2,1)} %get-tuple-element.51.xt, bf16[8,2,192,256]{3,2,1,0:T(8,128)(2,1)} %bitcast.21, bf16[128,768]{1,0:T(8,128)(2,1)} %bitcast.14, bf16[256,8448]{1,0:T(8,128)(2,1)} %get-tuple-element.53.dmat, ...), custom_call_target="tpu_custom_call" | custom-call | flops 5000000000 | bytes 30000000 | tf_op jit(solution)/shard_map/pallas_call | solution.py:603
  170.2 4.0 %shard_map.377 = (f32[16,768]{1,0:T(8,128)}, f32[96,2304]{1,0:T(8,128)}, f32[2,96]{1,0:T(2,128)}, f32[96,768]{1,0:T(8,128)}, f32[96]{0:T(128)}, /*index=5*/f32[2...) custom-call(bf16[16,2,96,384]{3,2,1,0:T(8,128)(2,1)} %bitcast.12, ...), custom_call_target="tpu_custom_call" | custom-call | tf_op jit(solution)/shard_map/pallas_call | solution.py:638

commit v2 on v1

v2 whole, which is shorter than its diff:
```python
import functools
import typing

import jax
import jax.numpy as jnp
from jax import lax
from jax.experimental import pallas as pl
from jax.experimental.pallas import tpu as pltpu
from jax.sharding import PartitionSpec as P

D = 768
HEADS = 12
HD = 64
FF = 3072
EPS = 1e-05
NEG = -1e30
BF = jnp.bfloat16
F32 = jnp.float32
MESH = pl.DeviceIdType.MESH
VMEM_LIMIT = 63 * 2**20

N_VEC = 17
R_SECOND, R_TOK, R_SMIX, R_FIRST, R_CMIX, R_ALL = 0, 768, 1536, 2304, 3072, 3840
PART = 384
SHARD = D // 8
PIECES = [("fo", i) for i in range(4)] + [("fi", i) for i in range(4)]
PIECES += [("co", 0), ("cq", 0), ("ckv", 0), ("ckv", 1), ("so", 0), ("qkv", 0), ("qkv", 1), ("qkv", 2)]
OPERANDS = ["fb"] * 4 + ["inner0", "inner1", "inner2", "inner3", "cb", "cq", "dkv0", "dkv1", "sb", "proj0", "proj1", "proj2"]
WAYS = "BABACBCBBABBABAB"
ORDER = (
    0, 1, 2, 100, 101, 102, 103, 104, 105, 3, 4, 5, 6, 7, 106, 200, 8, 201, 107, 9, 10, 11, 108, 204,
    202, 12, 203, 13, 14, 15, 16, 109, 300, 110, 205, 17, 302, 112, 18, 206, 19, 111, 304, 207, 20, 209, 301, 21,
    22, 305, 114, 115, 303, 208, 400, 306, 212, 402, 113, 401, 404, 23, 210, 403, 500, 307, 309, 502, 405, 211, 214, 409,
    312, 505, 308, 24, 407, 215, 406, 412, 310, 314, 507, 213, 408, 311, 501, 410, 504, 315, 503, 414, 411, 600, 508, 602,
    510, 313, 509, 415, 605, 511, 506, 413, 512, 515, 607, 514, 608, 513, 610, 611, 615, 613,
)
O_INNER, O_PROJ, O_SB, O_CQ, O_CB, O_FB, O_ALL = 0, 1536, 2688, 3072, 3456, 3840, 4608


class Columns(typing.NamedTuple):
    inner: int
    proj: int
    sb: int
    cq: int
    cb: int
    fb: int
    end: int


def columns(fast):
    return Columns(0, 0, 2304, 3072, 3840, 4608, 5376) if fast else Columns(0, 3072, 5376, 6144, 6912, 7680, 8448)


def dot(a, b):
    return lax.dot_general(a, b, (((1,), (0,)), ((), ())), preferred_element_type=F32)


def dot_nt(a, b):
    return lax.dot_general(a, b, (((1,), (1,)), ((), ())), preferred_element_type=F32)


def dot_tn(a, b):
    return lax.dot_general(a, b, (((0,), (0,)), ((), ())), preferred_element_type=F32)


def at(index, size):
    return pl.ds(pl.multiple_of(index * size, size), size)


def half_mask(half):
    lane = lax.broadcasted_iota(jnp.int32, (1, 2 * HD), 1)
    return ((lane >= HD) if half else (lane < HD)).astype(F32).astype(BF)


def total_row(values):
    return jnp.sum(values, axis=0, keepdims=True)


def gelu_and_slope(v):
    cdf = 0.5 * (1.0 + lax.erf(v * 0.7071067811865476))
    return v * cdf, cdf + v * (jnp.exp(-0.5 * v * v) * 0.3989422804014327)


def norm_rows(r):
    centered = r - jnp.mean(r, axis=-1, keepdims=True)
    rstd = lax.rsqrt(jnp.mean(centered * centered, axis=-1, keepdims=True) + EPS)
    return centered * rstd, rstd


def norm_rows_back(grad, xhat, rstd, gain):
    e = grad * gain
    mean_e = jnp.mean(e, axis=-1, keepdims=True)
    mean_x = jnp.mean(e * xhat, axis=-1, keepdims=True)
    return (e - mean_e - xhat * mean_x) * rstd


def attend(q_ref, k_ref, vt_ref, bias_ref, p_ref, mix_t_ref):
    scores = []
    for j in range(HEADS // 2):
        cols = slice(2 * HD * j, 2 * HD * (j + 1))
        q2, k2 = q_ref[:, cols], k_ref[:, cols]
        scores += [dot_nt(k2 * half_mask(half), q2) for half in range(2)]
    for h, st in enumerate(scores):
        st = st + bias_ref[...]
        e = jnp.exp(st - jnp.max(st, axis=0, keepdims=True))
        p_ref[h] = (e * (1.0 / jnp.sum(e, axis=0, keepdims=True))).astype(BF)
    for h in range(HEADS):
        rows = slice(HD * h, HD * (h + 1))
        mix_t_ref[rows, :] = dot(vt_ref[rows, :], p_ref[h]).astype(BF)


def attend_back(p_ref, dmix_ref, q_ref, v_ref, kt_ref, dq_t_ref, put, begin, end):
    parts = []
    for j in range(begin, end):
        cols = slice(2 * HD * j, 2 * HD * (j + 1))
        dm2, q2, v2 = dmix_ref[:, cols], q_ref[:, cols], v_ref[:, cols]
        parts += [(2 * j + half, dm2 * half_mask(half), q2 * half_mask(half), dot_nt(v2 * half_mask(half), dm2)) for half in range(2)]
    grads = []
    for h, dm, q, dp in parts:
        p = p_ref[h].astype(F32)
        t = p * dp
        grads.append((t - p * jnp.sum(t, axis=0, keepdims=True)).astype(BF))
    for n, (h, dm, q, dp) in enumerate(parts):
        dq_t_ref[HD * h : HD * (h + 1), :] = dot(kt_ref[HD * h : HD * (h + 1), :], grads[n]).astype(BF)
    for n in range(0, len(parts), 2):
        (h, dm0, q0, _), (_, dm1, q1, _) = parts[n : n + 2]
        put(h // 2, dot(grads[n], q0) + dot(grads[n + 1], q1), dot(p_ref[h], dm0) + dot(p_ref[h + 1], dm1))


class Refs:
    def __init__(self, names, refs):
        for name, ref in zip(names, refs, strict=True):
            setattr(self, name, ref)


class Inputs(typing.NamedTuple):
    tokens: typing.Any
    states: typing.Any
    retrieved: typing.Any
    live: typing.Any
    lengths: typing.Any
    self_bias: typing.Any
    self_out_bias: typing.Any
    norm1: typing.Any
    cq_bias: typing.Any
    cv_bias: typing.Any
    co_bias: typing.Any
    norm2: typing.Any
    fi_bias: typing.Any
    fo_bias: typing.Any
    norm3: typing.Any
    cotangent: typing.Any
    h_qkv: typing.Any
    h_qkv6: typing.Any
    h_so: typing.Any
    h_cq: typing.Any
    h_ckv: typing.Any
    h_co: typing.Any
    h_fi: typing.Any
    h_fo: typing.Any


INPUTS = list(Inputs._fields)


def layer(m, net, at_col):
    rows = m.tokens.shape[0]
    length = m.lengths[0, 0]
    scale = HD**-0.5
    xt, dmat, vec = m.xt, m.dmat, m.vec
    copies = {}
    order = [("qkv%d" % i, m.h_qkv6.at[:, :, :, :, i * PART : (i + 1) * PART], m.ring.at[i]) for i in range(6)]
    order += [("so", m.h_so, m.w_so), ("cq", m.h_cq, m.w_cq), ("ckv", m.h_ckv, m.w_ckv), ("co", m.h_co, m.w_co)]
    order += [("fi", m.h_fi, m.w_fi), ("fo", m.h_fo, m.w_fo)]
    for i, (name, src, dst) in enumerate(order):
        copies[name] = pltpu.make_async_copy(src, dst, m.w_sem.at[i])
        copies[name].start()
    if net:
        net.greet()

    def piece(name):
        return slice(getattr(at_col, name), getattr(at_col, name) + D)

    xt[R_TOK : R_TOK + D, :] = m.tokens[...].T
    key_at = lax.broadcasted_iota(jnp.int32, (rows, rows), 0)
    query_at = lax.broadcasted_iota(jnp.int32, (rows, rows), 1)
    m.bias_s[...] = jnp.where((key_at <= query_at) & (key_at < length), 0.0, NEG)
    if net:
        net.begin()
    topk = m.retrieved.shape[0]
    slots = m.bias_c.shape[0]
    slot_rank = lax.broadcasted_iota(jnp.int32, (topk, rows), 0)
    chosen = jnp.where((m.live[...] > 0) | (slot_rank == 0), m.retrieved[...], -1)

    def mask_rows(i, _):
        ids = lax.broadcasted_iota(jnp.int32, (32, rows), 0) + i * 32
        hit = jnp.zeros((32, rows), jnp.bool_)
        for j in range(topk):
            hit = hit | (ids == chosen[j : j + 1, :])
        m.bias_c[at(i, 32), :] = jnp.where(hit, 0.0, NEG)
        return 0

    lax.fori_loop(0, slots // 32, mask_rows, 0)

    for i, (ref, bias) in enumerate(((m.q, 0), (m.q, 0), (m.k, None), (m.k, None), (m.v, 1), (m.v, 1))):
        copies["qkv%d" % i].wait()
        cols = slice((i % 2) * PART, (i % 2 + 1) * PART)
        got = dot(m.tokens[...], m.ring[i].reshape(D, PART))
        if bias is not None:
            got = got + m.self_bias[bias : bias + 1, cols]
        got = got.astype(BF)
        ref[:, cols] = got * scale if bias == 0 else got
    m.vt[...] = m.v[...].T
    attend(m.q, m.k, m.vt, m.bias_s, m.p_s, xt.at[R_SMIX : R_SMIX + D])
    m.vt[...] = m.k[...].T * scale
    copies["so"].wait()
    if net:
        net.swap_rows("smix")
    m.mix_b[...] = xt[R_SMIX : R_SMIX + D, :].T
    m.acc[...] = dot(m.mix_b[...], m.w_so[...])

    def ln1(rs):
        xhat, rstd = norm_rows(m.tokens[rs, :].astype(F32) + m.acc[rs, :] + m.self_out_bias[...][None, :])
        m.xhat1[rs, :] = xhat
        m.rstd1[rs, :] = rstd
        m.sec_b[rs, :] = (xhat * m.norm1[0:1, :] + m.norm1[1:2, :]).astype(BF)

    ln1(slice(0, rows))
    xt[R_FIRST : R_FIRST + D, :] = m.sec_b[...].T
    if net:
        net.swap_rows("first")

    copies["cq"].wait()
    m.k[...] = (dot(m.sec_b[...], m.w_cq[...]) + m.cq_bias[...][None, :]).astype(BF) * scale
    copies["ckv"].wait()
    if net:
        net.have_states()
    states = m.all_states[...].reshape(slots, D)
    m.sk[...] = dot(states, m.w_ckv[:, :D]).astype(BF)
    m.sv[...] = (dot(states, m.w_ckv[:, D:]) + m.cv_bias[...][None, :]).astype(BF)
    m.svt[...] = m.sv[...].T
    attend(m.k, m.sk, m.svt, m.bias_c, m.p_c, xt.at[R_CMIX : R_CMIX + D])
    m.svt[...] = m.sk[...].T * scale
    copies["co"].wait()
    if net:
        net.swap_rows("cmix")
    m.mix_b[...] = xt[R_CMIX : R_CMIX + D, :].T
    m.acc[...] = dot(m.mix_b[...], m.w_co[...])

    def ln2(rs):
        first = m.xhat1[rs, :] * m.norm1[0:1, :] + m.norm1[1:2, :]
        xhat, rstd = norm_rows(first + m.acc[rs, :] + m.co_bias[...][None, :])
        m.xhat2[rs, :] = xhat
        m.rstd2[rs, :] = rstd
        m.sec_b[rs, :] = (xhat * m.norm2[0:1, :] + m.norm2[1:2, :]).astype(BF)

    ln2(slice(0, rows))
    xt[R_SECOND : R_SECOND + D, :] = m.sec_b[...].T
    if net:
        net.swap_rows("second")

    copies["fi"].wait()
    copies["fo"].wait()
    for j in range(FF // D):
        cols = slice(j * D, (j + 1) * D)
        m.acc2[...] = dot(m.sec_b[...], m.w_fi[:, cols])
        bias = m.fi_bias[cols][None, :]

        def gelu(rs):
            a, s = gelu_and_slope(m.acc2[rs, :] + bias)
            m.mix_b[rs, :] = a.astype(BF)
            m.slope[rs, cols] = s.astype(BF)

        gelu(slice(0, rows))
        m.act_t[2 * j : 2 * j + 2] = m.mix_b[...].T.reshape(2, 2, 2 * SHARD, rows)
        if net:
            net.swap_act(j)
        got = dot(m.mix_b[...], m.w_fo[cols, :])
        m.acc[...] = got if j == 0 else m.acc[...] + got

    def ln3(rs):
        second = m.xhat2[rs, :] * m.norm2[0:1, :] + m.norm2[1:2, :]
        xhat, rstd = norm_rows(second + m.acc[rs, :] + m.fo_bias[...][None, :])
        m.result[rs, :] = (xhat * m.norm3[0:1, :] + m.norm3[1:2, :]).astype(BF)
        place = lax.broadcasted_iota(jnp.int32, (rows, 1), 0)
        g = m.cotangent[rs, :].astype(F32) * jnp.where(place < length, 1.0, 0.0)
        d = norm_rows_back(g, xhat, rstd, m.norm3[0:1, :])
        m.d_res[rs, :] = d
        db = d.astype(BF)
        dmat[rs, piece("fb")] = db
        return total_row(g * xhat), total_row(g), total_row(db.astype(F32))

    vec[N_VEC:, :] = jnp.zeros((vec.shape[0] - N_VEC, D), F32)
    vec[11:12, :], vec[12:13, :], vec[10:11, :] = ln3(slice(0, rows))
    if net:
        net.swap("fb")

    steps = []

    def feed_back(j):
        cols = slice(j * D, (j + 1) * D)
        inner = slice(at_col.inner + j * D, at_col.inner + (j + 1) * D)
        m.acc2[...] = dot_nt(dmat[:, piece("fb")], m.w_fo[cols, :])

        def inner_rows(rs):
            d = (m.slope[rs, cols].astype(F32) * m.acc2[rs, :]).astype(BF)
            dmat[rs, inner] = d
            return total_row(d.astype(F32))

        vec[13 + j : 14 + j, :] = inner_rows(slice(0, rows))
        if net:
            net.swap("inner%d" % j)

    def feed_back_x(j):
        inner = slice(at_col.inner + j * D, at_col.inner + (j + 1) * D)
        got = dot_nt(dmat[:, inner], m.w_fi[:, j * D : (j + 1) * D])
        m.acc[...] = (m.d_res[...] if j == 0 else m.acc[...]) + got

    for j in range(FF // D):
        steps += [functools.partial(feed_back, j), functools.partial(feed_back_x, j)]

    def norm_back(xhat_ref, rstd_ref, norm, name):
        def block(rs):
            g, xhat = m.acc[rs, :], xhat_ref[rs, :]
            d = norm_rows_back(g, xhat, rstd_ref[rs, :], norm[0:1, :])
            m.d_res[rs, :] = d
            db = d.astype(BF)
            dmat[rs, piece(name)] = db
            return total_row(g * xhat), total_row(g), total_row(db.astype(F32))

        sums = block(slice(0, rows))
        if net:
            net.swap(name)
        return sums

    def back_norm2():
        copies["qkv"] = pltpu.make_async_copy(m.h_qkv, m.w_fi.at[:, 0 : 3 * D], m.w_sem.at[len(order)])
        copies["qkv"].start()
        vec[8:9, :], vec[9:10, :], vec[7:8, :] = norm_back(m.xhat2, m.rstd2, m.norm2, "cb")

    def back_cross_out():
        m.mix_b[...] = dot_nt(dmat[:, piece("cb")], m.w_co[...]).astype(BF)

    def put_store(j, dk, dv):
        cols = slice(2 * HD * j, 2 * HD * (j + 1))
        m.dkv[:, cols] = dk.astype(BF)
        m.dkv[:, D + 2 * HD * j : D + 2 * HD * (j + 1)] = dv.astype(BF)
        vec[6:7, cols] = total_row(dv)

    def back_cross(part):
        attend_back(m.p_c, m.mix_b, m.k, m.sv, m.svt, m.dqt, put_store, 2 * part, 2 * part + 2)
        if net and part == 2:
            net.swap("dkv0")
            net.swap("dkv1")

    def back_query():
        dq = m.dqt[...].T
        dmat[:, piece("cq")] = dq
        if net:
            net.swap("cq")
        vec[5:6, :] = total_row(dq.astype(F32))

    def back_store():
        m.dstore[...] = dot_nt(m.dkv[...], m.w_ckv[...]).astype(BF).reshape(m.dstore.shape)
        if net:
            net.send_dstore()

    def back_first():
        m.acc[...] = m.d_res[...] + dot_nt(dmat[:, piece("cq")], m.w_cq[...])

    def back_norm1():
        if net:
            net.inner_gone()
        vec[3:4, :], vec[4:5, :], vec[2:3, :] = norm_back(m.xhat1, m.rstd1, m.norm1, "sb")

    def back_self_out():
        m.mix_b[...] = dot_nt(dmat[:, piece("sb")], m.w_so[...]).astype(BF)

    def put_self(j, dk, dv):
        dvb = dv.astype(BF)
        begin = at_col.proj + D + 2 * HD * j
        dmat[:, begin : begin + 2 * HD] = dk.astype(BF)
        dmat[:, begin + D : begin + D + 2 * HD] = dvb
        vec[1:2, 2 * HD * j : 2 * HD * (j + 1)] = total_row(dvb.astype(F32))

    def back_self(part):
        attend_back(m.p_s, m.mix_b, m.q, m.v, m.vt, m.dqt, put_self, 2 * part, 2 * part + 2)
        if net and part == 2:
            net.swap("proj1")
            net.swap("proj2")

    def back_proj():
        dq = m.dqt[...].T
        dmat[:, at_col.proj : at_col.proj + D] = dq
        if net:
            net.swap("proj0")
        vec[0:1, :] = total_row(dq.astype(F32))
        if net:
            net.send_vec()

    def back_hidden():
        copies["qkv"].wait()
        m.acc[...] = m.d_res[...] + dot_nt(dmat[:, at_col.proj : at_col.proj + 3 * D], m.w_fi[:, 0 : 3 * D])
        if net:
            net.keep(m.acc, m.d_hidden)
            net.keep(m.result, m.result_out)

    steps += [back_norm2, back_cross_out] + [functools.partial(back_cross, part) for part in range(3)]
    steps += [back_query, back_store, back_first, back_norm1, back_self_out] + [functools.partial(back_self, part) for part in range(3)]
    steps += [back_proj, back_hidden]
    if net:
        steps += [net.small_sums, net.small_total]
        for number in ORDER:
            if number < 100:
                steps[number]()
            else:
                net.step(number // 100 - 1, number % 100)
        net.finish()
    else:
        for step in steps:
            step()


def weight_inputs(args):
    self_qkv, self_out, cross_q, cross_kv, cross_out, ffn_in, ffn_out = (args[i] for i in (5, 7, 10, 12, 14, 17, 19))
    return (self_qkv, self_qkv.reshape(4, 2, 2, D // 16, 3 * D), self_out, cross_q, cross_kv, cross_out, ffn_in, ffn_out)


def small_inputs(args):
    (hidden, store, retrieved, live, lengths, _, self_bias, _, self_out_bias, norm1, _, cross_q_bias,
     _, cross_v_bias, _, cross_out_bias, norm2, _, ffn_in_bias, _, ffn_out_bias, norm3, cotangent) = args
    return (
        hidden[0, 0], store[0], jnp.swapaxes(retrieved[0, 0], 0, 1), jnp.swapaxes(live[0, 0], 0, 1), lengths, self_bias,
        self_out_bias, norm1, cross_q_bias, cross_v_bias, cross_out_bias, norm2, ffn_in_bias, ffn_out_bias, norm3, cotangent[0, 0],
    )


def layer_scratch(rows, slots, ring):
    wide = (rows, D)
    return dict(
        ring=((ring, 4, 2, 2, D // 16, PART), BF), w_so=((D, D), BF), w_cq=((D, D), BF), w_ckv=((D, 2 * D), BF),
        w_co=((D, D), BF), w_fi=((D, FF), BF), w_fo=((FF, D), BF),
        q=(wide, BF), k=(wide, BF), v=(wide, BF), vt=((D, rows), BF), bias_s=((rows, rows), F32),
        p_s=((HEADS, rows, rows), BF), sk=((slots, D), BF), sv=((slots, D), BF), svt=((D, slots), BF),
        bias_c=((slots, rows), F32), p_c=((HEADS, slots, rows), BF), mix_b=(wide, BF),
        acc=(wide, F32), acc2=(wide, F32), xhat1=(wide, F32), xhat2=(wide, F32),
        sec_b=(wide, BF), slope=((rows, FF), BF), d_res=(wide, F32), dqt=((D, rows), BF),
        rstd1=((rows, 1), F32), rstd2=((rows, 1), F32),
    )


def buffers(table):
    return [pltpu.VMEM(dims, kind) for dims, kind in table.values()]


PLAIN_OUT = ["result", "acc", "xt", "act_t", "dmat", "dkv", "dstore", "vec"]


def plain_kernel(names, *refs):
    layer(Refs(names, refs), None, columns(False))


def run_plain(args, states_all):
    rows, slots = args[0].shape[2], states_all.shape[0]
    at_col = columns(False)
    table = layer_scratch(rows, slots, 6)
    del table["acc"]
    vmem, hbm, smem = (pl.BlockSpec(memory_space=s) for s in (pltpu.VMEM, pl.ANY, pltpu.SMEM))
    shape = jax.ShapeDtypeStruct
    names = INPUTS + PLAIN_OUT + list(table) + ["w_sem"]
    names[names.index("states")] = "all_states"
    small = small_inputs(args)
    outs = pl.pallas_call(
        functools.partial(plain_kernel, names),
        out_shape=(
            shape((rows, D), BF), shape((rows, D), F32), shape((R_ALL, rows), BF), shape((8, 2, 2 * SHARD, rows), BF),
            shape((rows, at_col.end), BF), shape((slots, 2 * D), BF), shape((slots, D), BF), shape((24, D), F32),
        ),
        in_specs=[vmem] * 4 + [smem] + [vmem] * 11 + [hbm] * 8,
        out_specs=(vmem,) * 8,
        scratch_shapes=buffers(table) + [pltpu.SemaphoreType.DMA((13,))],
        compiler_params=pltpu.CompilerParams(vmem_limit_bytes=VMEM_LIMIT),
    )(small[0], states_all, *small[2:], *weight_inputs(args))
    return outs


class Net:
    def __init__(self, m, at_col):
        self.m, self.at_col = m, at_col
        b, r = lax.axis_index("blk"), lax.axis_index("rep")
        self.b, self.r = b, r
        self.z, self.x, self.y, self.c = b // 2, b % 2, r // 2, r % 2
        z, x, y, c = self.z, self.x, self.y, self.c
        self.at_x = (z * 2 + 1 - x, r)
        self.at_y = (b, (1 - y) * 2 + c)
        self.at_c = (b, y * 2 + 1 - c)
        side = z // 2
        self.side, self.is_end = side, jnp.logical_or(z == 0, z == 3)
        self.at_mid, self.at_end = ((1 + side) * 2 + x, r), (3 * side * 2 + x, r)
        self.at_near, self.at_far = ((2 - side) * 2 + x, r), (3 * (1 - side) * 2 + x, r)
        self.at_blk = [(lax.rem(b + step, 8), r) for step in range(1, 8)]
        self.at_rep = [(b, lax.rem(r + step, 4)) for step in range(1, 4)]
        self.swaps, self.swap_count = {}, 0
        self.steps = {}
        self.sent, self.sent_end, self.sent_mid, self.locals, self.here = [], [], [], [], []
        self.cores = {i: [] for i in range(len(PIECES))}
        self.nth = {i: WAYS[:i].count(way) for i, way in enumerate(WAYS)}

    def copy(self, src, dst, s_sem, r_sem, device):
        return pltpu.make_async_remote_copy(
            src_ref=src, dst_ref=dst, send_sem=s_sem, recv_sem=r_sem, device_id=device, device_id_type=MESH
        )

    def send(self, *args):
        copy = self.copy(*args)
        copy.start()
        self.sent.append(copy)
        return copy

    def send_some(self, among, make):
        make().start()
        among.append(make)

    def greet(self):
        barrier = pltpu.get_barrier_semaphore()
        for device in self.at_blk + self.at_rep:
            pl.semaphore_signal(barrier, inc=1, device_id=device, device_id_type=MESH)

    def begin(self):
        m = self.m
        m.all_states[self.b] = m.states[...]
        pl.semaphore_wait(pltpu.get_barrier_semaphore(), len(self.at_blk) + len(self.at_rep))
        self.gather = []
        for i, device in enumerate(self.at_blk):
            self.gather.append(self.send(m.states, m.all_states.at[self.b], m.gs.at[i], m.gr.at[i], device))
        self.swap_rows("tok")

    def have_states(self):
        for copy in self.gather:
            copy.wait_recv()
        self.trade("states", self.m.all_states, self.m.states_p)

    def trade(self, name, src, dst):
        i = self.swap_count
        self.swap_count += 1
        self.swaps[name] = self.send(src, dst, self.m.os.at[i], self.m.orr.at[i], self.at_c)

    def need(self, *names):
        for name in names:
            if name not in self.here:
                self.swaps[name].wait_recv()
                self.here.append(name)

    def swap_rows(self, name):
        row = {"tok": R_TOK, "smix": R_SMIX, "first": R_FIRST, "cmix": R_CMIX, "second": R_SECOND}[name]
        self.trade(name, self.m.xt.at[row : row + D], self.m.xt_p.at[row : row + D])

    def swap_act(self, j):
        here = slice(2 * j, 2 * j + 2)
        self.trade("act%d" % j, self.m.act_t.at[here, 1 - self.c], self.m.act_p.at[here])

    def half(self, start, who):
        return pl.ds(pl.multiple_of(start + who * PART, 128), PART)

    def operand(self, name):
        m, at_col = self.m, self.at_col
        if name[:3] == "dkv":
            return m.dkv, int(name[3]) * D, m.dkv_p, int(name[3]) * PART
        if name[:5] == "inner":
            return m.dmat, at_col.inner + int(name[5]) * D, m.d_p, O_INNER + int(name[5]) * PART
        if name[:4] == "proj":
            return m.dmat, at_col.proj + int(name[4]) * D, m.d_p, O_PROJ + int(name[4]) * PART
        return m.dmat, getattr(at_col, name), m.d_p, {"sb": O_SB, "cq": O_CQ, "cb": O_CB}[name]

    def swap(self, name):
        m = self.m
        if name == "fb":
            start = self.at_col.fb
            self.trade("fb", m.dmat.at[:, start : start + D], m.d_p.at[:, O_FB : O_FB + D])
            return
        ref, start, there, place = self.operand(name)
        self.trade(name, ref.at[:, self.half(start, 1 - self.c)], there.at[:, place : place + PART])

    def product(self, i):
        m = self.m
        kind, part = PIECES[i]
        if kind == "fo":
            self.need("fb", *("act%d" % j for j in range(4)))
            up = slice((part // 2) * SHARD, (part // 2 + 1) * SHARD)
            left = m.act_t[:, self.c, up, :].reshape(D, -1)
            left_p = m.act_p[:, up, :].reshape(D, -1)
            begin = (part % 2) * PART
            right = m.dmat[:, self.at_col.fb + begin : self.at_col.fb + begin + PART]
            right_p = m.d_p[:, O_FB + begin : O_FB + begin + PART]
        else:
            name = OPERANDS[i]
            ref, start, there, place = self.operand(name)
            rows_of, row = {"fi": ("second", R_SECOND), "co": ("cmix", R_CMIX), "cq": ("first", R_FIRST), "ckv": ("states", 0),
                            "so": ("smix", R_SMIX), "qkv": ("tok", R_TOK)}[kind]
            self.need(rows_of, name)
            right = ref[:, self.half(start, self.c)]
            right_p = there[:, place : place + PART]
            if kind == "ckv":
                left = m.all_states[...].reshape(-1, D).T
                left_p = m.states_p[...].reshape(-1, D).T
            else:
                left, left_p = m.xt[row : row + D, :], m.xt_p[row : row + D, :]
        m.ring[i] = (dot(left, right) + dot(left_p, right_p)).astype(BF).reshape(4, 2, 2, SHARD // 2, PART)

    def step(self, stage, i):
        n = self.nth[i]
        if stage == 0:
            self.product(i)
        ways = {
            "A": (self.a0, self.a1, self.a2, self.a3, self.a4),
            "B": (self.b0, self.b1, self.b2, self.b3, self.b4, self.b5),
            "C": (self.c0, self.c1, self.c2, self.c3, self.c4),
        }
        ways[WAYS[i]][stage](i, n)

    def post(self, i, src, dst, device):
        n = len(self.steps.setdefault(i, []))
        self.steps[i].append(self.send(src, dst, self.m.ps.at[i, n], self.m.pr.at[i, n], device))

    def arrived(self, i):
        self.steps[i][-1].wait_recv()

    def z_send(self, i, part, zb):
        m, others, edge = self.m, pl.ds(1 - self.side, 3), 3 * self.side

        @pl.when(self.is_end)
        def _():
            self.send_some(self.sent_end, lambda: self.copy(part.at[others], zb, m.zs.at[i, 0], m.zr.at[i, 0], self.at_mid))

        @pl.when(jnp.logical_not(self.is_end))
        def _():
            self.send_some(self.sent_mid, lambda: self.copy(part.at[edge], zb.at[0], m.zs.at[i, 0], m.zr.at[i, 1], self.at_end))

    def z_pass(self, i, part, zb, zm):
        m, side = self.m, self.side
        others, far, near = pl.ds(1 - side, 3), 2 * (1 - side), 1

        @pl.when(jnp.logical_not(self.is_end))
        def _():
            self.copy(part.at[others], zb, m.zs.at[i, 0], m.zr.at[i, 0], self.at_end).wait_recv()
            zb[far] = zb[far] + part[3 * (1 - side)]
            self.send_some(self.sent_mid, lambda: self.copy(zb.at[far], zb.at[1], m.zs.at[i, 1], m.zr.at[i, 2], self.at_far))
            zb[near] = zb[near] + part[2 - side]
            self.send_some(self.sent_mid, lambda: self.copy(zb.at[near], zm, m.zs.at[i, 2], m.zr.at[i, 3], self.at_near))

    def z_sum(self, i, part, zb, zm, out):
        m, side = self.m, self.side

        @pl.when(self.is_end)
        def _():
            self.copy(part.at[0], zb.at[0], m.zs.at[i, 0], m.zr.at[i, 1], self.at_mid).wait_recv()
            self.copy(part.at[0], zb.at[1], m.zs.at[i, 0], m.zr.at[i, 2], self.at_near).wait_recv()
            out[...] = (part[self.z].astype(F32) + zb[0].astype(F32) + zb[1].astype(F32)).astype(BF)

        @pl.when(jnp.logical_not(self.is_end))
        def _():
            self.copy(part.at[0], zm, m.zs.at[i, 0], m.zr.at[i, 3], self.at_near).wait_recv()
            out[...] = (part[self.z].astype(F32) + zb[2 * side].astype(F32) + zm[...].astype(F32)).astype(BF)

    def last(self, i, ref, there):
        self.keep(ref, there)
        n = len(self.cores[i])
        self.cores[i].append(self.send(ref, there, self.m.cs.at[i, n], self.m.cr.at[i, n], self.at_c))

    def a0(self, i, n):
        self.post(i, self.m.ring.at[i, :, 1 - self.x], self.m.ax.at[n], self.at_x)

    def a1(self, i, n):
        m = self.m
        self.arrived(i)
        m.ax[n] = m.ax[n] + m.ring[i, :, self.x]
        self.z_send(i, m.ax.at[n], m.azb.at[n])

    def a2(self, i, n):
        self.z_pass(i, self.m.ax.at[n], self.m.azb.at[n], self.m.azm.at[n])

    def a3(self, i, n):
        m = self.m
        self.z_sum(i, m.ax.at[n], m.azb.at[n], m.azm.at[n], m.ah.at[n])
        self.post(i, m.ah.at[n], m.ay.at[n], self.at_y)

    def a4(self, i, n):
        m = self.m
        self.arrived(i)
        m.ay[n] = m.ay[n] + m.ah[n]
        self.last(i, m.ay.at[n], m.fin.at[i, self.c])

    def b0(self, i, n):
        self.post(i, self.m.ring.at[i, :, :, 1 - self.y], self.m.by.at[n], self.at_y)

    def b1(self, i, n):
        m = self.m
        self.arrived(i)
        m.by[n] = m.by[n] + m.ring[i, :, :, self.y]
        self.post(i, m.by.at[n, :, 1 - self.x], m.bx.at[n], self.at_x)

    def b2(self, i, n):
        m = self.m
        self.arrived(i)
        m.bx[n] = m.bx[n] + m.by[n, :, self.x]
        self.z_send(i, m.bx.at[n], m.bzb.at[n])

    def b3(self, i, n):
        self.z_pass(i, self.m.bx.at[n], self.m.bzb.at[n], self.m.bzm.at[n])

    def b4(self, i, n):
        m = self.m
        self.z_sum(i, m.bx.at[n], m.bzb.at[n], m.bzm.at[n], m.bh.at[n])
        self.post(i, m.bh.at[n], m.bg.at[n], self.at_y)
        self.last(i, m.bh.at[n], m.fin.at[i, self.c, self.y])

    def b5(self, i, n):
        self.arrived(i)
        self.last(i, self.m.bg.at[n], self.m.fin.at[i, self.c, 1 - self.y])

    def c0(self, i, n):
        self.z_send(i, self.m.ring.at[i], self.m.czb.at[n])

    def c1(self, i, n):
        self.z_pass(i, self.m.ring.at[i], self.m.czb.at[n], self.m.czm.at[n])

    def c2(self, i, n):
        m = self.m
        self.z_sum(i, m.ring.at[i], m.czb.at[n], m.czm.at[n], m.ch.at[n])
        self.post(i, m.ch.at[n, 1 - self.x], m.cx.at[n], self.at_x)

    def c3(self, i, n):
        m = self.m
        self.arrived(i)
        m.cx[n] = m.cx[n] + m.ch[n, self.x]
        self.post(i, m.cx.at[n], m.cy.at[n], self.at_y)

    def c4(self, i, n):
        m = self.m
        self.arrived(i)
        m.cy[n] = m.cy[n] + m.cx[n]
        self.last(i, m.cy.at[n], m.fin.at[i, self.c])

    def keep(self, src, dst):
        copy = pltpu.make_async_copy(src, dst, self.m.fs.at[len(self.locals)])
        copy.start()
        self.locals.append(copy)

    def inner_gone(self):
        for j in range(4):
            self.swaps["inner%d" % j].wait_send()

    def send_dstore(self):
        m = self.m
        self.small_d = [
            self.send(m.dstore.at[device[0]], m.ds_in.at[i], m.dss.at[i], m.dsr.at[i], device) for i, device in enumerate(self.at_blk)
        ]

    def send_vec(self):
        m, vec = self.m, self.m.vec
        m.vsh[...] = jnp.zeros(m.vsh.shape, F32)
        for s in range(8):
            m.vsh[s, 0:13, 0:SHARD] = vec[0:13, s * SHARD : (s + 1) * SHARD]
            for part in range(4):
                begin = 4 * SHARD * s + SHARD * part
                row, col = 13 + begin // D, begin % D
                m.vsh[s, 13 + part : 14 + part, 0:SHARD] = vec[row : row + 1, col : col + SHARD]
        self.small_v = [
            self.send(m.vsh.at[device[0]], m.vin.at[i], m.vss.at[i], m.vsr.at[i], device) for i, device in enumerate(self.at_blk)
        ]

    def finish(self):
        for copies in self.cores.values():
            for copy in copies:
                copy.wait_recv()
        for name, copy in self.swaps.items():
            if name not in self.here:
                copy.wait_recv()
        gone = [self.swaps["inner%d" % j] for j in range(4)]
        for copy in self.sent:
            if not any(copy is other for other in gone):
                copy.wait_send()

        @pl.when(self.is_end)
        def _():
            for make in self.sent_end:
                make().wait_send()

        @pl.when(jnp.logical_not(self.is_end))
        def _():
            for make in self.sent_mid:
                make().wait_send()

        for copy in self.locals:
            copy.wait()

    def small_total(self):
        m = self.m
        for copy in self.small:
            copy.wait_recv()
        m.vec_out[...] = (m.vrep[0] + m.vrep[1]) + (m.vrep[2] + m.vrep[3])

    def small_sums(self):
        m = self.m
        total = m.dstore[self.b].astype(F32)
        for i, copy in enumerate(self.small_d):
            copy.wait_recv()
            total = total + m.ds_in[i].astype(F32)
        m.dstore_out[...] = total
        total = m.vsh[self.b]
        for i, copy in enumerate(self.small_v):
            copy.wait_recv()
            total = total + m.vin[i]
        m.vrep[self.r] = total
        self.small = [
            self.send(m.vrep.at[self.r], m.vrep.at[self.r], m.vps.at[i], m.vpr.at[i], device)
            for i, device in enumerate(self.at_rep)
        ]


SUM_OUT = ["result_out", "d_hidden", "fin", "dstore_out", "vec_out"]


def sum_kernel(names, *refs):
    m, at_col = Refs(names, refs), columns(True)
    layer(m, Net(m, at_col), at_col)


def run_sum(args):
    rows, own = args[0].shape[2], args[1].shape[1]
    slots = 8 * own
    n, half = len(PIECES), SHARD // 2
    na, nb, nc = (WAYS.count(way) for way in "ABC")
    table = layer_scratch(rows, slots, n)
    table.update(
        result=((rows, D), BF), xt=((R_ALL, rows), BF), xt_p=((R_ALL, rows), BF), act_t=((8, 2, 2 * SHARD, rows), BF),
        act_p=((8, 2 * SHARD, rows), BF), dmat=((rows, columns(True).end), BF), d_p=((rows, O_ALL), BF),
        dkv=((slots, 2 * D), BF), dkv_p=((slots, D), BF), dstore=((8, own, D), BF), vec=((24, D), F32),
        all_states=((8, own, D), BF), states_p=((8, own, D), BF),
        ax=((na, 4, 2, half, PART), BF), azb=((na, 3, 2, half, PART), BF), azm=((na, 2, half, PART), BF),
        ah=((na, 2, half, PART), BF), ay=((na, 2, half, PART), BF),
        by=((nb, 4, 2, half, PART), BF), bx=((nb, 4, half, PART), BF), bzb=((nb, 3, half, PART), BF),
        bzm=((nb, half, PART), BF), bh=((nb, half, PART), BF), bg=((nb, half, PART), BF),
        czb=((nc, 3, 2, 2, half, PART), BF), czm=((nc, 2, 2, half, PART), BF), ch=((nc, 2, 2, half, PART), BF),
        cx=((nc, 2, half, PART), BF), cy=((nc, 2, half, PART), BF), ds_in=((7, own, D), BF),
        vsh=((8, 24, 128), F32), vin=((7, 24, 128), F32), vrep=((4, 24, 128), F32),
    )
    sems = dict(
        w_sem=(13,), gs=(7,), gr=(7,), os=(24,), orr=(24,), ps=(n, 3), pr=(n, 3), zs=(n, 3), zr=(n, 4),
        cs=(n, 2), cr=(n, 2), fs=(2 * n + 2,), dss=(7,), dsr=(7,), vss=(7,), vsr=(7,), vps=(3,), vpr=(3,),
    )
    vmem, hbm, smem = (pl.BlockSpec(memory_space=s) for s in (pltpu.VMEM, pl.ANY, pltpu.SMEM))
    shape = jax.ShapeDtypeStruct
    return pl.pallas_call(
        functools.partial(sum_kernel, INPUTS + SUM_OUT + list(table) + list(sems)),
        out_shape=(
            shape((rows, D), BF), shape((rows, D), F32), shape((n, 2, 2, half, PART), BF), shape((own, D), F32), shape((24, 128), F32),
        ),
        in_specs=[vmem] * 4 + [smem] + [vmem] * 11 + [hbm] * 8,
        out_specs=(hbm, hbm, hbm, vmem, vmem),
        scratch_shapes=buffers(table) + [pltpu.SemaphoreType.DMA(dims) for dims in sems.values()],
        compiler_params=pltpu.CompilerParams(collective_id=0, has_side_effects=True, vmem_limit_bytes=VMEM_LIMIT),
        cost_estimate=pl.CostEstimate(flops=15 * 10**9, bytes_accessed=5 * 10**7, transcendentals=10**6),
    )(*small_inputs(args), *weight_inputs(args))


def place_kernel(result, d_hidden, fin, dstore, vec, *outs):
    (o_result, o_hidden, o_dstore, o_qkv, o_sbias, o_so, o_sob, o_n1, o_cq, o_cqb, o_ckv, o_cvb, o_co, o_cob, o_n2, o_fi, o_fib, o_fo, o_fob, o_n3) = outs
    o_result[...] = result[...]
    o_hidden[...] = d_hidden[...]
    o_dstore[...] = dstore[...]
    wide = {"qkv": o_qkv, "so": o_so, "cq": o_cq, "ckv": o_ckv, "co": o_co, "fi": o_fi}
    for i, (kind, part) in enumerate(PIECES):
        for c in range(2):
            values = fin[i, c].astype(F32)
            if kind == "fo":
                begin = c * 2 * SHARD + (part // 2) * SHARD
                o_fo[begin : begin + SHARD, (part % 2) * PART : (part % 2 + 1) * PART] = values
            else:
                ref = wide[kind]
                begin = part * D + c * PART
                ref[:, begin : begin + PART] = values
    for ref, row in ((o_sbias, 0), (o_n1, 3), (o_n2, 8), (o_n3, 11)):
        ref[...] = vec[row : row + 2, 0:SHARD]
    for ref, row in ((o_sob, 2), (o_cqb, 5), (o_cvb, 6), (o_cob, 7), (o_fob, 10)):
        ref[...] = vec[row, 0:SHARD]
    for part in range(4):
        o_fib[pl.ds(part * SHARD, SHARD)] = vec[13 + part, 0:SHARD]


def place(result, d_hidden, fin, dstore, vec):
    shape = lambda *dims: jax.ShapeDtypeStruct(dims, F32)
    return pl.pallas_call(
        place_kernel,
        out_shape=(
            jax.ShapeDtypeStruct(result.shape, BF), shape(*d_hidden.shape), shape(*dstore.shape), shape(SHARD, 3 * D), shape(2, SHARD), shape(SHARD, D), shape(SHARD), shape(2, SHARD),
            shape(SHARD, D), shape(SHARD), shape(SHARD, 2 * D), shape(SHARD), shape(SHARD, D), shape(SHARD), shape(2, SHARD),
            shape(SHARD, FF), shape(FF // 8), shape(FF // 8, D), shape(SHARD), shape(2, SHARD),
        ),
        compiler_params=pltpu.CompilerParams(vmem_limit_bytes=VMEM_LIMIT),
    )(result, d_hidden, fin.reshape(len(PIECES), 2, SHARD, PART), dstore, vec)


def sum_plainly(states, xt, act_t, dmat, dkv, dstore, vec):
    def total(value, dim):
        part = lax.psum_scatter(value, "blk", scatter_dimension=dim, tiled=True)
        return lax.psum(part.astype(BF), "rep").astype(F32)

    at_col = columns(False)

    def rows_of(start):
        return lax.slice_in_dim(xt, start, start + D, axis=0)

    def cols_of(start, width):
        return lax.slice_in_dim(dmat, start, start + width, axis=1)

    g_qkv = total(dot(rows_of(R_TOK), cols_of(at_col.proj, 3 * D)), 0)
    g_so = total(dot(rows_of(R_SMIX), cols_of(at_col.sb, D)), 0)
    g_cq = total(dot(rows_of(R_FIRST), cols_of(at_col.cq, D)), 0)
    g_co = total(dot(rows_of(R_CMIX), cols_of(at_col.cb, D)), 0)
    g_fi = total(dot(rows_of(R_SECOND), cols_of(at_col.inner, FF)), 0)
    g_fo = total(dot(act_t.reshape(FF, -1), cols_of(at_col.fb, D)), 0)
    g_ckv = total(dot_tn(states, dkv), 0)
    g_store = lax.psum_scatter(dstore.astype(F32), "blk", scatter_dimension=0, tiled=True)
    g_fib = total(vec[13:N_VEC].reshape(FF), 0)
    v = total(vec[:13].T, 0)
    two = lambda row: v[:, row : row + 2].T
    return (
        g_store, g_qkv, two(0), g_so, v[:, 2], two(3), g_cq, v[:, 5], g_ckv, v[:, 6], g_co, v[:, 7], two(8),
        g_fi, g_fib, g_fo, v[:, 10], two(11),
    )


def on_device(fast, *args):
    if fast:
        result, d_hidden, *grads = place(*run_sum(args))
    else:
        states_all = lax.all_gather(args[1][0], "blk", axis=0, tiled=True)
        result, d_hidden, *operands = run_plain(args, states_all)
        grads = sum_plainly(states_all, *operands)
    return (result[None, None], d_hidden[None, None], grads[0][None], *grads[1:])


def solution(mesh):
    fast = mesh.shape["blk"] == 8 and mesh.shape["rep"] == 4
    deep, flat = P("rep", "blk", None, None), P("rep", "blk", None)
    in_specs = (deep, flat, deep, deep, P("rep", "blk")) + (P(),) * 17 + (deep,)
    w, vec, two = P("blk", None), P("blk"), P(None, "blk")
    out_specs = (deep, deep, flat, w, two, w, vec, two, w, vec, w, vec, w, vec, two, w, vec, w, vec, two)
    return jax.shard_map(
        functools.partial(on_device, fast), mesh=mesh, in_specs=in_specs, out_specs=out_specs, check_vma=False
    )
```

time: 175 us -> 118 us (0.67)
  Pallas kernels: 168 us -> 116 us
  local copies, waits for them, and re-layouts: 4.5 us -> 0 us
    pallas_call x4 -> x2, Pallas kernels: 168 us -> 116 us  [the longest x1 111 us: run_sum(): pl.pallas_call(functools.partial(sum_kernel, INPUTS + SUM_OUT + list(tabl...]
    unnamed x2 -> x0, local copies, waits for them, and re-layouts: 3.19 us -> none
where the time goes in v2:
time: 118 us; the launch traced here: 117 us
  Pallas kernels  116 us (98%)
  between operations  1.5 us (1%)
    pallas_call x1, Pallas kernels, run_sum(): pl.pallas_call(functools.partial(sum_kernel, INPUTS + SUM_OUT + list(tabl...  111 us
    pallas_call x1, Pallas kernels, place(): pl.pallas_call(place_kernel, out_shape=(jax.ShapeDtypeStruct(result.shape...  4.75 us

profile of v2, /device:TPU:0, one launch (start us, length us, event | category | flops | bytes accessed | tf_op | source)
XLA Modules:
  0.0 117.4 jit_solution(8911116308652986723)
XLA Ops:
  1.3 111.2 %shard_map.374 = (bf16[256,768]{1,0:T(8,128)(2,1)}, f32[256,768]{1,0:T(8,128)}, bf16[16,2,2,48,384]{4,3,2,1,0:T(8,128)(2,1)}, f32[16,768]{1,0:T(8,128)}, f32[24,128]{1,0:T(8,128)}) custom-call(bf16[256,768]{1,0:T(8,128)(2,1)} %bitcast.17, bf16[16,768]{1,0:T(8,128)(2,1)} %bitcast.23, s32[64,256]{1,0:T(8,128)} %bitcast.20, s32[64,256]{1,0:T(8,128)} %bitcast.21, ...), custom_call_target="tpu_custom_call" | custom-call | flops 15000000512 | bytes 50000000 | tf_op jit(solution)/shard_map/pallas_call | solution.py:854
  112.5 4.7 %shard_map.375 = (bf16[256,768]{1,0:T(8,128)(2,1)}, f32[256,768]{1,0:T(8,128)}, f32[16,768]{1,0:T(8,128)}, f32[96,2304]{1,0:T(8,128)}, f32[2,96]{1,0:T(2,128)}, ...) custom-call(bf16[256,768]{1,0:T(8,128)(2,1)} %get-tuple-element.45.r, ...), custom_call_target="tpu_custom_call" | custom-call | tf_op jit(solution)/shard_map/pallas_call | solution.py:893

commit v3 on v2

--- a/solution.py
+++ b/solution.py
@@ -23,16 +23,20 @@
 R_SECOND, R_TOK, R_SMIX, R_FIRST, R_CMIX, R_ALL = 0, 768, 1536, 2304, 3072, 3840
 PART = 384
 SHARD = D // 8
-PIECES = [("fo", i) for i in range(4)] + [("fi", i) for i in range(4)]
-PIECES += [("co", 0), ("cq", 0), ("ckv", 0), ("ckv", 1), ("so", 0), ("qkv", 0), ("qkv", 1), ("qkv", 2)]
-OPERANDS = ["fb"] * 4 + ["inner0", "inner1", "inner2", "inner3", "cb", "cq", "dkv0", "dkv1", "sb", "proj0", "proj1", "proj2"]
-WAYS = "BABACBCBBABBABAB"
+PRODUCTS = [("fo", i) for i in range(4)] + [("fi", i) for i in range(4)]
+PRODUCTS += [("co", 0), ("cq", 0), ("ckv", 0), ("ckv", 1), ("so", 0), ("qkv", 0), ("qkv", 1), ("qkv", 2)]
+LANES = 128
+UNITS = PART // LANES
+PIECES = [(i, 0, UNITS) for i in range(12)] + [(i, unit, 1) for i in range(12, 16) for unit in range(UNITS)]
+WAYS = "BCAACABBBBABABBBCBAAABBB"
 ORDER = (
-    0, 1, 2, 100, 101, 102, 103, 104, 105, 3, 4, 5, 6, 7, 106, 200, 8, 201, 107, 9, 10, 11, 108, 204,
-    202, 12, 203, 13, 14, 15, 16, 109, 300, 110, 205, 17, 302, 112, 18, 206, 19, 111, 304, 207, 20, 209, 301, 21,
-    22, 305, 114, 115, 303, 208, 400, 306, 212, 402, 113, 401, 404, 23, 210, 403, 500, 307, 309, 502, 405, 211, 214, 409,
-    312, 505, 308, 24, 407, 215, 406, 412, 310, 314, 507, 213, 408, 311, 501, 410, 504, 315, 503, 414, 411, 600, 508, 602,
-    510, 313, 509, 415, 605, 511, 506, 413, 512, 515, 607, 514, 608, 513, 610, 611, 615, 613,
+    0, 1, 2, 3, 4, 5, 6, 101, 102, 100, 103, 7, 107, 106, 104, 8, 9, 10, 11, 105, 12, 13, 14, 15,
+    16, 17, 18, 108, 19, 20, 21, 22, 110, 202, 200, 201, 122, 116, 203, 207, 111, 204, 205, 301, 23, 206, 109, 302,
+    210, 120, 208, 113, 216, 304, 222, 123, 300, 402, 24, 303, 307, 114, 316, 401, 119, 211, 121, 305, 306, 403, 220, 115,
+    112, 209, 310, 405, 308, 213, 400, 117, 404, 322, 223, 416, 407, 410, 502, 118, 219, 406, 500, 214, 320, 507, 501, 311,
+    506, 408, 221, 212, 422, 420, 503, 319, 309, 215, 508, 313, 411, 522, 505, 419, 323, 312, 217, 218, 409, 511, 314, 504,
+    413, 412, 516, 321, 423, 315, 510, 318, 317, 600, 509, 414, 607, 513, 421, 523, 606, 415, 520, 417, 418, 608, 622, 514,
+    519, 521, 611, 515, 512, 517, 609, 613, 623, 518, 614, 621, 615, 617,
 )
 O_INNER, O_PROJ, O_SB, O_CQ, O_CB, O_FB, O_ALL = 0, 1536, 2688, 3072, 3456, 3840, 4608
 
@@ -169,12 +173,24 @@
     scale = HD**-0.5
     xt, dmat, vec = m.xt, m.dmat, m.vec
     copies = {}
-    order = [("qkv%d" % i, m.h_qkv6.at[:, :, :, :, i * PART : (i + 1) * PART], m.ring.at[i]) for i in range(6)]
-    order += [("so", m.h_so, m.w_so), ("cq", m.h_cq, m.w_cq), ("ckv", m.h_ckv, m.w_ckv), ("co", m.h_co, m.w_co)]
-    order += [("fi", m.h_fi, m.w_fi), ("fo", m.h_fo, m.w_fo)]
+    order = [("so", m.h_so, m.w_so), ("cq", m.h_cq, m.w_cq), ("ckv", m.h_ckv, m.w_ckv), ("co", m.h_co, m.w_co), ("fi", m.h_fi, m.w_fi)]
+
+    def fetch_units(src, first, count, sem):
+        for i in range(count):
+            pltpu.make_async_copy(src(i), m.ring.at[first + i], sem).start()
+
+    def have_units(first, count, sem):
+        here = m.ring.at[first : first + count]
+        pltpu.make_async_copy(here, here, sem).wait()
+
+    def weight(slot):
+        return jnp.concatenate([m.ring[UNITS * slot + unit].reshape(D, LANES) for unit in range(UNITS)], axis=1)
+
+    fetch_units(lambda i: m.h_qkv6.at[:, :, :, :, i * LANES : (i + 1) * LANES], 0, 18, m.w_sem.at[6])
     for i, (name, src, dst) in enumerate(order):
         copies[name] = pltpu.make_async_copy(src, dst, m.w_sem.at[i])
         copies[name].start()
+    fetch_units(lambda i: m.h_fo.at[i // 6, :, :, :, :, i % 6 * LANES : (i % 6 + 1) * LANES], 24, 24, m.w_sem.at[7])
     if net:
         net.greet()
 
@@ -203,9 +219,10 @@
     lax.fori_loop(0, slots // 32, mask_rows, 0)
 
     for i, (ref, bias) in enumerate(((m.q, 0), (m.q, 0), (m.k, None), (m.k, None), (m.v, 1), (m.v, 1))):
-        copies["qkv%d" % i].wait()
+        if i == 0:
+            have_units(0, 18, m.w_sem.at[6])
         cols = slice((i % 2) * PART, (i % 2 + 1) * PART)
-        got = dot(m.tokens[...], m.ring[i].reshape(D, PART))
+        got = dot(m.tokens[...], weight(i))
         if bias is not None:
             got = got + m.self_bias[bias : bias + 1, cols]
         got = got.astype(BF)
@@ -260,7 +277,7 @@
         net.swap_rows("second")
 
     copies["fi"].wait()
-    copies["fo"].wait()
+    have_units(24, 24, m.w_sem.at[7])
     for j in range(FF // D):
         cols = slice(j * D, (j + 1) * D)
         m.acc2[...] = dot(m.sec_b[...], m.w_fi[:, cols])
@@ -275,8 +292,10 @@
         m.act_t[2 * j : 2 * j + 2] = m.mix_b[...].T.reshape(2, 2, 2 * SHARD, rows)
         if net:
             net.swap_act(j)
-        got = dot(m.mix_b[...], m.w_fo[cols, :])
-        m.acc[...] = got if j == 0 else m.acc[...] + got
+        for part in range(2):
+            got = dot(m.mix_b[...], weight(8 + 2 * j + part))
+            here = slice(part * PART, (part + 1) * PART)
+            m.acc[:, here] = got if j == 0 else m.acc[:, here] + got
 
     def ln3(rs):
         second = m.xhat2[rs, :] * m.norm2[0:1, :] + m.norm2[1:2, :]
@@ -300,7 +319,8 @@
     def feed_back(j):
         cols = slice(j * D, (j + 1) * D)
         inner = slice(at_col.inner + j * D, at_col.inner + (j + 1) * D)
-        m.acc2[...] = dot_nt(dmat[:, piece("fb")], m.w_fo[cols, :])
+        left, right = (dmat[:, at_col.fb + part * PART : at_col.fb + (part + 1) * PART] for part in range(2))
+        m.acc2[...] = dot_nt(left, weight(8 + 2 * j)) + dot_nt(right, weight(9 + 2 * j))
 
         def inner_rows(rs):
             d = (m.slope[rs, cols].astype(F32) * m.acc2[rs, :]).astype(BF)
@@ -309,7 +329,7 @@
 
         vec[13 + j : 14 + j, :] = inner_rows(slice(0, rows))
         if net:
-            net.swap("inner%d" % j)
+            net.swap("inner", j)
 
     def feed_back_x(j):
         inner = slice(at_col.inner + j * D, at_col.inner + (j + 1) * D)
@@ -334,7 +354,7 @@
         return sums
 
     def back_norm2():
-        copies["qkv"] = pltpu.make_async_copy(m.h_qkv, m.w_fi.at[:, 0 : 3 * D], m.w_sem.at[len(order)])
+        copies["qkv"] = pltpu.make_async_copy(m.h_qkv, m.w_fi.at[:, 0 : 3 * D], m.w_sem.at[5])
         copies["qkv"].start()
         vec[8:9, :], vec[9:10, :], vec[7:8, :] = norm_back(m.xhat2, m.rstd2, m.norm2, "cb")
 
@@ -350,8 +370,8 @@
     def back_cross(part):
         attend_back(m.p_c, m.mix_b, m.k, m.sv, m.svt, m.dqt, put_store, 2 * part, 2 * part + 2)
         if net and part == 2:
-            net.swap("dkv0")
-            net.swap("dkv1")
+            net.swap("dkv", 0)
+            net.swap("dkv", 1)
 
     def back_query():
         dq = m.dqt[...].T
@@ -386,14 +406,14 @@
     def back_self(part):
         attend_back(m.p_s, m.mix_b, m.q, m.v, m.vt, m.dqt, put_self, 2 * part, 2 * part + 2)
         if net and part == 2:
-            net.swap("proj1")
-            net.swap("proj2")
+            net.swap("proj", 1)
+            net.swap("proj", 2)
 
     def back_proj():
         dq = m.dqt[...].T
         dmat[:, at_col.proj : at_col.proj + D] = dq
         if net:
-            net.swap("proj0")
+            net.swap("proj", 0)
         vec[0:1, :] = total_row(dq.astype(F32))
         if net:
             net.send_vec()
@@ -402,14 +422,15 @@
         copies["qkv"].wait()
         m.acc[...] = m.d_res[...] + dot_nt(dmat[:, at_col.proj : at_col.proj + 3 * D], m.w_fi[:, 0 : 3 * D])
         if net:
-            net.keep(m.acc, m.d_hidden)
-            net.keep(m.result, m.result_out)
+            net.keep(m.acc, m.d_hidden, m.fs.at[1])
+            net.keep(m.result, m.result_out, m.fs.at[2])
 
     steps += [back_norm2, back_cross_out] + [functools.partial(back_cross, part) for part in range(3)]
     steps += [back_query, back_store, back_first, back_norm1, back_self_out] + [functools.partial(back_self, part) for part in range(3)]
     steps += [back_proj, back_hidden]
     if net:
         steps += [net.small_sums, net.small_total]
+        steps += [functools.partial(net.make, i) for i in range(len(PRODUCTS))]
         for number in ORDER:
             if number < 100:
                 steps[number]()
@@ -423,7 +444,8 @@
 
 def weight_inputs(args):
     self_qkv, self_out, cross_q, cross_kv, cross_out, ffn_in, ffn_out = (args[i] for i in (5, 7, 10, 12, 14, 17, 19))
-    return (self_qkv, self_qkv.reshape(4, 2, 2, D // 16, 3 * D), self_out, cross_q, cross_kv, cross_out, ffn_in, ffn_out)
+    return (self_qkv, self_qkv.reshape(4, 2, 2, D // 16, 3 * D), self_out, cross_q, cross_kv, cross_out, ffn_in,
+            ffn_out.reshape(FF // D, 4, 2, 2, D // 16, D))
 
 
 def small_inputs(args):
@@ -435,11 +457,11 @@
     )
 
 
-def layer_scratch(rows, slots, ring):
+def layer_scratch(rows, slots):
     wide = (rows, D)
     return dict(
-        ring=((ring, 4, 2, 2, D // 16, PART), BF), w_so=((D, D), BF), w_cq=((D, D), BF), w_ckv=((D, 2 * D), BF),
-        w_co=((D, D), BF), w_fi=((D, FF), BF), w_fo=((FF, D), BF),
+        ring=((UNITS * 16, 4, 2, 2, D // 16, LANES), BF), w_so=((D, D), BF), w_cq=((D, D), BF), w_ckv=((D, 2 * D), BF),
+        w_co=((D, D), BF), w_fi=((D, FF), BF),
         q=(wide, BF), k=(wide, BF), v=(wide, BF), vt=((D, rows), BF), bias_s=((rows, rows), F32),
         p_s=((HEADS, rows, rows), BF), sk=((slots, D), BF), sv=((slots, D), BF), svt=((D, slots), BF),
         bias_c=((slots, rows), F32), p_c=((HEADS, slots, rows), BF), mix_b=(wide, BF),
@@ -463,7 +485,7 @@
 def run_plain(args, states_all):
     rows, slots = args[0].shape[2], states_all.shape[0]
     at_col = columns(False)
-    table = layer_scratch(rows, slots, 6)
+    table = layer_scratch(rows, slots)
     del table["acc"]
     vmem, hbm, smem = (pl.BlockSpec(memory_space=s) for s in (pltpu.VMEM, pl.ANY, pltpu.SMEM))
     shape = jax.ShapeDtypeStruct
@@ -478,7 +500,7 @@
         ),
         in_specs=[vmem] * 4 + [smem] + [vmem] * 11 + [hbm] * 8,
         out_specs=(vmem,) * 8,
-        scratch_shapes=buffers(table) + [pltpu.SemaphoreType.DMA((13,))],
+        scratch_shapes=buffers(table) + [pltpu.SemaphoreType.DMA((8,))],
         compiler_params=pltpu.CompilerParams(vmem_limit_bytes=VMEM_LIMIT),
     )(small[0], states_all, *small[2:], *weight_inputs(args))
     return outs
@@ -500,11 +522,14 @@
         self.at_near, self.at_far = ((2 - side) * 2 + x, r), (3 * (1 - side) * 2 + x, r)
         self.at_blk = [(lax.rem(b + step, 8), r) for step in range(1, 8)]
         self.at_rep = [(b, lax.rem(r + step, 4)) for step in range(1, 4)]
-        self.swaps, self.swap_count = {}, 0
-        self.steps = {}
-        self.sent, self.sent_end, self.sent_mid, self.locals, self.here = [], [], [], [], []
-        self.cores = {i: [] for i in range(len(PIECES))}
-        self.nth = {i: WAYS[:i].count(way) for i, way in enumerate(WAYS)}
+        self.here, self.swapped = [], []
+        self.steps, self.chain = {}, []
+        self.span, self.own, taken = [], [], dict.fromkeys(WAYS, 0)
+        for way, (product, unit, units) in zip(WAYS, PIECES, strict=True):
+            self.span.append(slice(taken[way], taken[way] + units))
+            self.own.append(slice(UNITS * product + unit, UNITS * product + unit + units))
+            taken[way] += units
+        self.made = []
 
     def copy(self, src, dst, s_sem, r_sem, device):
         return pltpu.make_async_remote_copy(
@@ -514,12 +539,10 @@
     def send(self, *args):
         copy = self.copy(*args)
         copy.start()
-        self.sent.append(copy)
         return copy
 
-    def send_some(self, among, make):
-        make().start()
-        among.append(make)
+    def sized(self, ref, s_sem, r_sem):
+        return self.copy(ref, ref, s_sem, r_sem, self.at_c)
 
     def greet(self):
         barrier = pltpu.get_barrier_semaphore()
@@ -530,62 +553,69 @@
         m = self.m
         m.all_states[self.b] = m.states[...]
         pl.semaphore_wait(pltpu.get_barrier_semaphore(), len(self.at_blk) + len(self.at_rep))
-        self.gather = []
-        for i, device in enumerate(self.at_blk):
-            self.gather.append(self.send(m.states, m.all_states.at[self.b], m.gs.at[i], m.gr.at[i], device))
+        for device in self.at_blk:
+            self.send(m.states, m.all_states.at[self.b], m.ss.at[0], m.sr.at[0], device)
         self.swap_rows("tok")
 
     def have_states(self):
-        for copy in self.gather:
-            copy.wait_recv()
-        self.trade("states", self.m.all_states, self.m.states_p)
+        m = self.m
+        self.sized(m.all_states.at[0:7], m.ss.at[0], m.sr.at[0]).wait_recv()
+        self.trade("states", m.all_states, m.states_p)
+
+    def group(self, name):
+        m = self.m
+        part = lambda start, width: m.d_p.at[:, start : start + width]
+        table = {
+            "rows": m.xt_p, "act": m.act_p, "fb": part(O_FB, D), "inner": part(O_INNER, 4 * PART), "cb": part(O_CB, PART),
+            "cq": part(O_CQ, PART), "dkv": m.dkv_p, "sb": part(O_SB, PART), "proj": part(O_PROJ, 3 * PART), "states": m.states_p,
+        }
+        i = list(table).index(name)
+        return table[name], m.os.at[i], m.orr.at[i]
 
     def trade(self, name, src, dst):
-        i = self.swap_count
-        self.swap_count += 1
-        self.swaps[name] = self.send(src, dst, self.m.os.at[i], self.m.orr.at[i], self.at_c)
+        _, s_sem, r_sem = self.group(name)
+        self.send(src, dst, s_sem, r_sem, self.at_c)
+        if name not in self.swapped:
+            self.swapped.append(name)
 
     def need(self, *names):
         for name in names:
             if name not in self.here:
-                self.swaps[name].wait_recv()
+                self.sized(*self.group(name)).wait_recv()
                 self.here.append(name)
 
     def swap_rows(self, name):
         row = {"tok": R_TOK, "smix": R_SMIX, "first": R_FIRST, "cmix": R_CMIX, "second": R_SECOND}[name]
-        self.trade(name, self.m.xt.at[row : row + D], self.m.xt_p.at[row : row + D])
+        self.trade("rows", self.m.xt.at[row : row + D], self.m.xt_p.at[row : row + D])
 
     def swap_act(self, j):
         here = slice(2 * j, 2 * j + 2)
-        self.trade("act%d" % j, self.m.act_t.at[here, 1 - self.c], self.m.act_p.at[here])
+        self.trade("act", self.m.act_t.at[here, 1 - self.c], self.m.act_p.at[here])
 
     def half(self, start, who):
         return pl.ds(pl.multiple_of(start + who * PART, 128), PART)
 
-    def operand(self, name):
+    def operand(self, name, part):
         m, at_col = self.m, self.at_col
-        if name[:3] == "dkv":
-            return m.dkv, int(name[3]) * D, m.dkv_p, int(name[3]) * PART
-        if name[:5] == "inner":
-            return m.dmat, at_col.inner + int(name[5]) * D, m.d_p, O_INNER + int(name[5]) * PART
-        if name[:4] == "proj":
-            return m.dmat, at_col.proj + int(name[4]) * D, m.d_p, O_PROJ + int(name[4]) * PART
-        return m.dmat, getattr(at_col, name), m.d_p, {"sb": O_SB, "cq": O_CQ, "cb": O_CB}[name]
-
-    def swap(self, name):
+        if name == "dkv":
+            return m.dkv, part * D, m.dkv_p, part * PART
+        place = {"inner": O_INNER, "proj": O_PROJ, "sb": O_SB, "cq": O_CQ, "cb": O_CB}[name]
+        return m.dmat, getattr(at_col, name) + part * D, m.d_p, place + part * PART
+
+    def swap(self, name, part=0):
         m = self.m
         if name == "fb":
             start = self.at_col.fb
             self.trade("fb", m.dmat.at[:, start : start + D], m.d_p.at[:, O_FB : O_FB + D])
             return
-        ref, start, there, place = self.operand(name)
+        ref, start, there, place = self.operand(name, part)
         self.trade(name, ref.at[:, self.half(start, 1 - self.c)], there.at[:, place : place + PART])
 
     def product(self, i):
         m = self.m
-        kind, part = PIECES[i]
+        kind, part = PRODUCTS[i]
         if kind == "fo":
-            self.need("fb", *("act%d" % j for j in range(4)))
+            self.need("fb", "act")
             up = slice((part // 2) * SHARD, (part // 2 + 1) * SHARD)
             left = m.act_t[:, self.c, up, :].reshape(D, -1)
             left_p = m.act_p[:, up, :].reshape(D, -1)
@@ -593,11 +623,10 @@
             right = m.dmat[:, self.at_col.fb + begin : self.at_col.fb + begin + PART]
             right_p = m.d_p[:, O_FB + begin : O_FB + begin + PART]
         else:
-            name = OPERANDS[i]
-            ref, start, there, place = self.operand(name)
-            rows_of, row = {"fi": ("second", R_SECOND), "co": ("cmix", R_CMIX), "cq": ("first", R_FIRST), "ckv": ("states", 0),
-                            "so": ("smix", R_SMIX), "qkv": ("tok", R_TOK)}[kind]
-            self.need(rows_of, name)
+            name, row = {"fi": ("inner", R_SECOND), "co": ("cb", R_CMIX), "cq": ("cq", R_FIRST), "ckv": ("dkv", 0),
+                         "so": ("sb", R_SMIX), "qkv": ("proj", R_TOK)}[kind]
+            self.need(name, "states" if kind == "ckv" else "rows")
+            ref, start, there, place = self.operand(name, part)
             right = ref[:, self.half(start, self.c)]
             right_p = there[:, place : place + PART]
             if kind == "ckv":
@@ -605,22 +634,30 @@
                 left_p = m.states_p[...].reshape(-1, D).T
             else:
                 left, left_p = m.xt[row : row + D, :], m.xt_p[row : row + D, :]
-        m.ring[i] = (dot(left, right) + dot(left_p, right_p)).astype(BF).reshape(4, 2, 2, SHARD // 2, PART)
+        total = (dot(left, right) + dot(left_p, right_p)).astype(BF)
+        for unit in range(UNITS):
+            m.ring[UNITS * i + unit] = total[:, unit * LANES : (unit + 1) * LANES].reshape(4, 2, 2, SHARD // 2, LANES)
+
+    def make(self, i):
+        if i not in self.made:
+            self.made.append(i)
+            self.product(i)
 
     def step(self, stage, i):
-        n = self.nth[i]
         if stage == 0:
-            self.product(i)
+            self.make(PIECES[i][0])
         ways = {
             "A": (self.a0, self.a1, self.a2, self.a3, self.a4),
             "B": (self.b0, self.b1, self.b2, self.b3, self.b4, self.b5),
             "C": (self.c0, self.c1, self.c2, self.c3, self.c4),
         }
-        ways[WAYS[i]][stage](i, n)
+        ways[WAYS[i]][stage](i, self.span[i], self.own[i])
 
     def post(self, i, src, dst, device):
-        n = len(self.steps.setdefault(i, []))
-        self.steps[i].append(self.send(src, dst, self.m.ps.at[i, n], self.m.pr.at[i, n], device))
+        sent = self.steps.setdefault(i, [])
+        if sent:
+            sent[-1].wait_send()
+        sent.append(self.send(src, dst, self.m.ps.at[i], self.m.pr.at[i, len(sent)], device))
 
     def arrived(self, i):
         self.steps[i][-1].wait_recv()
@@ -630,131 +667,129 @@
 
         @pl.when(self.is_end)
         def _():
-            self.send_some(self.sent_end, lambda: self.copy(part.at[others], zb, m.zs.at[i, 0], m.zr.at[i, 0], self.at_mid))
+            self.send(part.at[:, others], zb, m.zs.at[i], m.zr.at[i, 0], self.at_mid)
 
         @pl.when(jnp.logical_not(self.is_end))
         def _():
-            self.send_some(self.sent_mid, lambda: self.copy(part.at[edge], zb.at[0], m.zs.at[i, 0], m.zr.at[i, 1], self.at_end))
+            self.send(part.at[:, edge], zb.at[:, 0], m.zs.at[i], m.zr.at[i, 0], self.at_end)
 
     def z_pass(self, i, part, zb, zm):
         m, side = self.m, self.side
-        others, far, near = pl.ds(1 - side, 3), 2 * (1 - side), 1
+        far, near = 2 * (1 - side), 1
 
         @pl.when(jnp.logical_not(self.is_end))
         def _():
-            self.copy(part.at[others], zb, m.zs.at[i, 0], m.zr.at[i, 0], self.at_end).wait_recv()
-            zb[far] = zb[far] + part[3 * (1 - side)]
-            self.send_some(self.sent_mid, lambda: self.copy(zb.at[far], zb.at[1], m.zs.at[i, 1], m.zr.at[i, 2], self.at_far))
-            zb[near] = zb[near] + part[2 - side]
-            self.send_some(self.sent_mid, lambda: self.copy(zb.at[near], zm, m.zs.at[i, 2], m.zr.at[i, 3], self.at_near))
+            self.sized(zb, m.zs.at[i], m.zr.at[i, 0]).wait_recv()
+            zb[:, far] = zb[:, far] + part[:, 3 * (1 - side)]
+            self.send(zb.at[:, far], zb.at[:, 1], m.zs.at[i], m.zr.at[i, 1], self.at_far)
+            zb[:, near] = zb[:, near] + part[:, 2 - side]
+            self.send(zb.at[:, near], zm, m.zs.at[i], m.zr.at[i, 1], self.at_near)
 
     def z_sum(self, i, part, zb, zm, out):
         m, side = self.m, self.side
 
         @pl.when(self.is_end)
         def _():
-            self.copy(part.at[0], zb.at[0], m.zs.at[i, 0], m.zr.at[i, 1], self.at_mid).wait_recv()
-            self.copy(part.at[0], zb.at[1], m.zs.at[i, 0], m.zr.at[i, 2], self.at_near).wait_recv()
-            out[...] = (part[self.z].astype(F32) + zb[0].astype(F32) + zb[1].astype(F32)).astype(BF)
+            self.sized(zm, m.zs.at[i], m.zr.at[i, 0]).wait_recv()
+            self.sized(zm, m.zs.at[i], m.zr.at[i, 1]).wait_recv()
+            out[...] = (part[:, self.z].astype(F32) + zb[:, 0].astype(F32) + zb[:, 1].astype(F32)).astype(BF)
 
         @pl.when(jnp.logical_not(self.is_end))
         def _():
-            self.copy(part.at[0], zm, m.zs.at[i, 0], m.zr.at[i, 3], self.at_near).wait_recv()
-            out[...] = (part[self.z].astype(F32) + zb[2 * side].astype(F32) + zm[...].astype(F32)).astype(BF)
-
-    def last(self, i, ref, there):
-        self.keep(ref, there)
-        n = len(self.cores[i])
-        self.cores[i].append(self.send(ref, there, self.m.cs.at[i, n], self.m.cr.at[i, n], self.at_c))
-
-    def a0(self, i, n):
-        self.post(i, self.m.ring.at[i, :, 1 - self.x], self.m.ax.at[n], self.at_x)
-
-    def a1(self, i, n):
+            self.sized(zm, m.zs.at[i], m.zr.at[i, 1]).wait_recv()
+            out[...] = (part[:, self.z].astype(F32) + zb[:, 2 * side].astype(F32) + zm[...].astype(F32)).astype(BF)
+
+        self.chain.append((zb, i))
+
+    def last(self, ref, there):
+        m = self.m
+        pltpu.make_async_copy(ref, there, m.fs.at[0]).start()
+        self.send(ref, there, m.cs.at[0], m.cr.at[0], self.at_c)
+
+    def a0(self, i, at, own):
+        self.post(i, self.m.ring.at[own, :, 1 - self.x], self.m.ax.at[at], self.at_x)
+
+    def a1(self, i, at, own):
         m = self.m
         self.arrived(i)
-        m.ax[n] = m.ax[n] + m.ring[i, :, self.x]
-        self.z_send(i, m.ax.at[n], m.azb.at[n])
-
-    def a2(self, i, n):
-        self.z_pass(i, self.m.ax.at[n], self.m.azb.at[n], self.m.azm.at[n])
-
-    def a3(self, i, n):
-        m = self.m
-        self.z_sum(i, m.ax.at[n], m.azb.at[n], m.azm.at[n], m.ah.at[n])
-        self.post(i, m.ah.at[n], m.ay.at[n], self.at_y)
-
-    def a4(self, i, n):
+        m.ax[at] = m.ax[at] + m.ring[own, :, self.x]
+        self.z_send(i, m.ax.at[at], m.azb.at[at])
+
+    def a2(self, i, at, own):
+        self.z_pass(i, self.m.ax.at[at], self.m.azb.at[at], self.m.azm.at[at])
+
+    def a3(self, i, at, own):
+        m = self.m
+        self.z_sum(i, m.ax.at[at], m.azb.at[at], m.azm.at[at], m.ah.at[at])
+        self.post(i, m.ah.at[at], m.ay.at[at], self.at_y)
+
+    def a4(self, i, at, own):
         m = self.m
         self.arrived(i)
-        m.ay[n] = m.ay[n] + m.ah[n]
-        self.last(i, m.ay.at[n], m.fin.at[i, self.c])
-
-    def b0(self, i, n):
-        self.post(i, self.m.ring.at[i, :, :, 1 - self.y], self.m.by.at[n], self.at_y)
-
-    def b1(self, i, n):
+        m.ay[at] = m.ay[at] + m.ah[at]
+        self.last(m.ay.at[at], m.fin.at[own, self.c])
+
+    def b0(self, i, at, own):
+        self.post(i, self.m.ring.at[own, :, :, 1 - self.y], self.m.by.at[at], self.at_y)
+
+    def b1(self, i, at, own):
         m = self.m
         self.arrived(i)
-        m.by[n] = m.by[n] + m.ring[i, :, :, self.y]
-        self.post(i, m.by.at[n, :, 1 - self.x], m.bx.at[n], self.at_x)
-
-    def b2(self, i, n):
+        m.by[at] = m.by[at] + m.ring[own, :, :, self.y]
+        self.post(i, m.by.at[at, :, 1 - self.x], m.bx.at[at], self.at_x)
+
+    def b2(self, i, at, own):
         m = self.m
         self.arrived(i)
-        m.bx[n] = m.bx[n] + m.by[n, :, self.x]
-        self.z_send(i, m.bx.at[n], m.bzb.at[n])
-
-    def b3(self, i, n):
-        self.z_pass(i, self.m.bx.at[n], self.m.bzb.at[n], self.m.bzm.at[n])
-
-    def b4(self, i, n):
-        m = self.m
-        self.z_sum(i, m.bx.at[n], m.bzb.at[n], m.bzm.at[n], m.bh.at[n])
-        self.post(i, m.bh.at[n], m.bg.at[n], self.at_y)
-        self.last(i, m.bh.at[n], m.fin.at[i, self.c, self.y])
-
-    def b5(self, i, n):
+        m.bx[at] = m.bx[at] + m.by[at, :, self.x]
+        self.z_send(i, m.bx.at[at], m.bzb.at[at])
+
+    def b3(self, i, at, own):
+        self.z_pass(i, self.m.bx.at[at], self.m.bzb.at[at], self.m.bzm.at[at])
+
+    def b4(self, i, at, own):
+        m = self.m
+        self.z_sum(i, m.bx.at[at], m.bzb.at[at], m.bzm.at[at], m.bh.at[at])
+        self.post(i, m.bh.at[at], m.bg.at[at], self.at_y)
+        self.last(m.bh.at[at], m.fin.at[own, self.c, self.y])
+
+    def b5(self, i, at, own):
         self.arrived(i)
-        self.last(i, self.m.bg.at[n], self.m.fin.at[i, self.c, 1 - self.y])
-
-    def c0(self, i, n):
-        self.z_send(i, self.m.ring.at[i], self.m.czb.at[n])
-
-    def c1(self, i, n):
-        self.z_pass(i, self.m.ring.at[i], self.m.czb.at[n], self.m.czm.at[n])
-
-    def c2(self, i, n):
-        m = self.m
-        self.z_sum(i, m.ring.at[i], m.czb.at[n], m.czm.at[n], m.ch.at[n])
-        self.post(i, m.ch.at[n, 1 - self.x], m.cx.at[n], self.at_x)
-
-    def c3(self, i, n):
+        self.last(self.m.bg.at[at], self.m.fin.at[own, self.c, 1 - self.y])
+
+    def c0(self, i, at, own):
+        self.z_send(i, self.m.ring.at[own], self.m.czb.at[at])
+
+    def c1(self, i, at, own):
+        self.z_pass(i, self.m.ring.at[own], self.m.czb.at[at], self.m.czm.at[at])
+
+    def c2(self, i, at, own):
+        m = self.m
+        self.z_sum(i, m.ring.at[own], m.czb.at[at], m.czm.at[at], m.ch.at[at])
+        self.post(i, m.ch.at[at, 1 - self.x], m.cx.at[at], self.at_x)
+
+    def c3(self, i, at, own):
         m = self.m
         self.arrived(i)
-        m.cx[n] = m.cx[n] + m.ch[n, self.x]
-        self.post(i, m.cx.at[n], m.cy.at[n], self.at_y)
-
-    def c4(self, i, n):
+        m.cx[at] = m.cx[at] + m.ch[at, self.x]
+        self.post(i, m.cx.at[at], m.cy.at[at], self.at_y)
+
+    def c4(self, i, at, own):
         m = self.m
         self.arrived(i)
-        m.cy[n] = m.cy[n] + m.cx[n]
-        self.last(i, m.cy.at[n], m.fin.at[i, self.c])
-
-    def keep(self, src, dst):
-        copy = pltpu.make_async_copy(src, dst, self.m.fs.at[len(self.locals)])
-        copy.start()
-        self.locals.append(copy)
+        m.cy[at] = m.cy[at] + m.cx[at]
+        self.last(m.cy.at[at], m.fin.at[own, self.c])
+
+    def keep(self, src, dst, sem):
+        pltpu.make_async_copy(src, dst, sem).start()
 
     def inner_gone(self):
-        for j in range(4):
-            self.swaps["inner%d" % j].wait_send()
+        self.sized(*self.group("inner")).wait_send()
 
     def send_dstore(self):
         m = self.m
-        self.small_d = [
-            self.send(m.dstore.at[device[0]], m.ds_in.at[i], m.dss.at[i], m.dsr.at[i], device) for i, device in enumerate(self.at_blk)
-        ]
+        for i, device in enumerate(self.at_blk):
+            self.send(m.dstore.at[device[0]], m.ds_in.at[i], m.ss.at[1], m.sr.at[1], device)
 
     def send_vec(self):
         m, vec = self.m, self.m.vec
@@ -765,57 +800,46 @@
                 begin = 4 * SHARD * s + SHARD * part
                 row, col = 13 + begin // D, begin % D
                 m.vsh[s, 13 + part : 14 + part, 0:SHARD] = vec[row : row + 1, col : col + SHARD]
-        self.small_v = [
-            self.send(m.vsh.at[device[0]], m.vin.at[i], m.vss.at[i], m.vsr.at[i], device) for i, device in enumerate(self.at_blk)
-        ]
+        for i, device in enumerate(self.at_blk):
+            self.send(m.vsh.at[device[0]], m.vin.at[i], m.ss.at[2], m.sr.at[2], device)
 
     def finish(self):
-        for copies in self.cores.values():
-            for copy in copies:
-                copy.wait_recv()
-        for name, copy in self.swaps.items():
-            if name not in self.here:
-                copy.wait_recv()
-        gone = [self.swaps["inner%d" % j] for j in range(4)]
-        for copy in self.sent:
-            if not any(copy is other for other in gone):
-                copy.wait_send()
-
-        @pl.when(self.is_end)
-        def _():
-            for make in self.sent_end:
-                make().wait_send()
-
-        @pl.when(jnp.logical_not(self.is_end))
-        def _():
-            for make in self.sent_mid:
-                make().wait_send()
-
-        for copy in self.locals:
-            copy.wait()
+        m = self.m
+        for name in self.swapped:
+            self.need(name)
+            if name != "inner":
+                self.sized(*self.group(name)).wait_send()
+        for sent in self.steps.values():
+            sent[-1].wait_send()
+        for zb, i in self.chain:
+            self.sized(zb, m.zs.at[i], m.zr.at[i, 0]).wait_send()
+        for k, ref in enumerate((m.all_states.at[0:7], m.ds_in, m.vin, m.vrep.at[0:3])):
+            self.sized(ref, m.ss.at[k], m.sr.at[k]).wait_send()
+        half = m.fin.at[:, self.c]
+        self.sized(half, m.cs.at[0], m.cr.at[0]).wait()
+        pltpu.make_async_copy(half, half, m.fs.at[0]).wait()
+        pltpu.make_async_copy(m.acc, m.d_hidden, m.fs.at[1]).wait()
+        pltpu.make_async_copy(m.result, m.result_out, m.fs.at[2]).wait()
 
     def small_total(self):
         m = self.m
-        for copy in self.small:
-            copy.wait_recv()
+        self.sized(m.vrep.at[0:3], m.ss.at[3], m.sr.at[3]).wait_recv()
         m.vec_out[...] = (m.vrep[0] + m.vrep[1]) + (m.vrep[2] + m.vrep[3])
 
     def small_sums(self):
         m = self.m
+        self.sized(m.ds_in, m.ss.at[1], m.sr.at[1]).wait_recv()
         total = m.dstore[self.b].astype(F32)
-        for i, copy in enumerate(self.small_d):
-            copy.wait_recv()
+        for i in range(7):
             total = total + m.ds_in[i].astype(F32)
         m.dstore_out[...] = total
+        self.sized(m.vin, m.ss.at[2], m.sr.at[2]).wait_recv()
         total = m.vsh[self.b]
-        for i, copy in enumerate(self.small_v):
-            copy.wait_recv()
+        for i in range(7):
             total = total + m.vin[i]
         m.vrep[self.r] = total
-        self.small = [
-            self.send(m.vrep.at[self.r], m.vrep.at[self.r], m.vps.at[i], m.vpr.at[i], device)
-            for i, device in enumerate(self.at_rep)
-        ]
+        for device in self.at_rep:
+            self.send(m.vrep.at[self.r], m.vrep.at[self.r], m.ss.at[3], m.sr.at[3], device)
 
 
 SUM_OUT = ["result_out", "d_hidden", "fin", "dstore_out", "vec_out"]
@@ -830,31 +854,30 @@
     rows, own = args[0].shape[2], args[1].shape[1]
     slots = 8 * own
     n, half = len(PIECES), SHARD // 2
-    na, nb, nc = (WAYS.count(way) for way in "ABC")
-    table = layer_scratch(rows, slots, n)
+    na, nb, nc = (sum(piece[2] for piece, its in zip(PIECES, WAYS, strict=True) if its == way) for way in "ABC")
+    table = layer_scratch(rows, slots)
     table.update(
         result=((rows, D), BF), xt=((R_ALL, rows), BF), xt_p=((R_ALL, rows), BF), act_t=((8, 2, 2 * SHARD, rows), BF),
         act_p=((8, 2 * SHARD, rows), BF), dmat=((rows, columns(True).end), BF), d_p=((rows, O_ALL), BF),
         dkv=((slots, 2 * D), BF), dkv_p=((slots, D), BF), dstore=((8, own, D), BF), vec=((24, D), F32),
         all_states=((8, own, D), BF), states_p=((8, own, D), BF),
-        ax=((na, 4, 2, half, PART), BF), azb=((na, 3, 2, half, PART), BF), azm=((na, 2, half, PART), BF),
-        ah=((na, 2, half, PART), BF), ay=((na, 2, half, PART), BF),
-        by=((nb, 4, 2, half, PART), BF), bx=((nb, 4, half, PART), BF), bzb=((nb, 3, half, PART), BF),
-        bzm=((nb, half, PART), BF), bh=((nb, half, PART), BF), bg=((nb, half, PART), BF),
-        czb=((nc, 3, 2, 2, half, PART), BF), czm=((nc, 2, 2, half, PART), BF), ch=((nc, 2, 2, half, PART), BF),
-        cx=((nc, 2, half, PART), BF), cy=((nc, 2, half, PART), BF), ds_in=((7, own, D), BF),
+        ax=((na, 4, 2, half, LANES), BF), azb=((na, 3, 2, half, LANES), BF), azm=((na, 2, half, LANES), BF),
+        ah=((na, 2, half, LANES), BF), ay=((na, 2, half, LANES), BF),
+        by=((nb, 4, 2, half, LANES), BF), bx=((nb, 4, half, LANES), BF), bzb=((nb, 3, half, LANES), BF),
+        bzm=((nb, half, LANES), BF), bh=((nb, half, LANES), BF), bg=((nb, half, LANES), BF),
+        czb=((nc, 3, 2, 2, half, LANES), BF), czm=((nc, 2, 2, half, LANES), BF), ch=((nc, 2, 2, half, LANES), BF),
+        cx=((nc, 2, half, LANES), BF), cy=((nc, 2, half, LANES), BF), ds_in=((7, own, D), BF),
         vsh=((8, 24, 128), F32), vin=((7, 24, 128), F32), vrep=((4, 24, 128), F32),
     )
     sems = dict(
-        w_sem=(13,), gs=(7,), gr=(7,), os=(24,), orr=(24,), ps=(n, 3), pr=(n, 3), zs=(n, 3), zr=(n, 4),
-        cs=(n, 2), cr=(n, 2), fs=(2 * n + 2,), dss=(7,), dsr=(7,), vss=(7,), vsr=(7,), vps=(3,), vpr=(3,),
+        w_sem=(8,), ss=(4,), sr=(4,), os=(10,), orr=(10,), ps=(n,), pr=(n, 3), zs=(n,), zr=(n, 2), cs=(1,), cr=(1,), fs=(3,)
     )
     vmem, hbm, smem = (pl.BlockSpec(memory_space=s) for s in (pltpu.VMEM, pl.ANY, pltpu.SMEM))
     shape = jax.ShapeDtypeStruct
     return pl.pallas_call(
         functools.partial(sum_kernel, INPUTS + SUM_OUT + list(table) + list(sems)),
         out_shape=(
-            shape((rows, D), BF), shape((rows, D), F32), shape((n, 2, 2, half, PART), BF), shape((own, D), F32), shape((24, 128), F32),
+            shape((rows, D), BF), shape((rows, D), F32), shape((UNITS * 16, 2, 2, half, LANES), BF), shape((own, D), F32), shape((24, 128), F32),
         ),
         in_specs=[vmem] * 4 + [smem] + [vmem] * 11 + [hbm] * 8,
         out_specs=(hbm, hbm, hbm, vmem, vmem),
@@ -870,9 +893,9 @@
     o_hidden[...] = d_hidden[...]
     o_dstore[...] = dstore[...]
     wide = {"qkv": o_qkv, "so": o_so, "cq": o_cq, "ckv": o_ckv, "co": o_co, "fi": o_fi}
-    for i, (kind, part) in enumerate(PIECES):
+    for i, (kind, part) in enumerate(PRODUCTS):
         for c in range(2):
-            values = fin[i, c].astype(F32)
+            values = jnp.concatenate([fin[UNITS * i + unit, c] for unit in range(UNITS)], axis=1).astype(F32)
             if kind == "fo":
                 begin = c * 2 * SHARD + (part // 2) * SHARD
                 o_fo[begin : begin + SHARD, (part % 2) * PART : (part % 2 + 1) * PART] = values
@@ -898,7 +921,7 @@
             shape(SHARD, FF), shape(FF // 8), shape(FF // 8, D), shape(SHARD), shape(2, SHARD),
         ),
         compiler_params=pltpu.CompilerParams(vmem_limit_bytes=VMEM_LIMIT),
-    )(result, d_hidden, fin.reshape(len(PIECES), 2, SHARD, PART), dstore, vec)
+    )(result, d_hidden, fin.reshape(UNITS * len(PRODUCTS), 2, SHARD, LANES), dstore, vec)
 
 
 def sum_plainly(states, xt, act_t, dmat, dkv, dstore, vec):

time: 118 us -> 115 us (0.975)
  Pallas kernels: 116 us -> 113 us
    pallas_call x1, Pallas kernels: 111 us -> 108 us  [run_sum(): pl.pallas_call(functools.partial(sum_kernel, INPUTS + SUM_OUT + list(tabl...]
where the time goes in v3:
time: 115 us
  Pallas kernels  113 us (98%)
  between operations  1.5 us (1%)
    pallas_call x1, Pallas kernels, run_sum(): pl.pallas_call(functools.partial(sum_kernel, INPUTS + SUM_OUT + list(tabl...  108 us
    pallas_call x1, Pallas kernels, place(): pl.pallas_call(place_kernel, out_shape=(jax.ShapeDtypeStruct(result.shape...  4.73 us

profile of v3, /device:TPU:0, one launch (start us, length us, event | category | flops | bytes accessed | tf_op | source)
XLA Modules:
  0.0 114.6 jit_solution(14805864414706985273)
XLA Ops:
  1.3 108.4 %shard_map.374 = (bf16[256,768]{1,0:T(8,128)(2,1)}, f32[256,768]{1,0:T(8,128)}, bf16[48,2,2,48,128]{4,3,2,1,0:T(8,128)(2,1)}, f32[16,768]{1,0:T(8,128)}, f32[24,128]{1,0:T(8,128)}) custom-call(bf16[256,768]{1,0:T(8,128)(2,1)} %bitcast.19, bf16[16,768]{1,0:T(8,128)(2,1)} %bitcast.25, s32[64,256]{1,0:T(8,128)} %bitcast.22, s32[64,256]{1,0:T(8,128)} %bitcast.23, ...), custom_call_target="tpu_custom_call" | custom-call | flops 15000000512 | bytes 50000000 | tf_op jit(solution)/shard_map/pallas_call | solution.py:877
  109.7 4.7 %shard_map.375 = (bf16[256,768]{1,0:T(8,128)(2,1)}, f32[256,768]{1,0:T(8,128)}, f32[16,768]{1,0:T(8,128)}, f32[96,2304]{1,0:T(8,128)}, f32[2,96]{1,0:T(2,128)}, ...) custom-call(bf16[256,768]{1,0:T(8,128)(2,1)} %get-tuple-element.45.r, ...), custom_call_target="tpu_custom_call" | custom-call | tf_op jit(solution)/shard_map/pallas_call | solution.py:916

commit v4 on v3

--- a/solution.py
+++ b/solution.py
@@ -30,7 +30,7 @@
 PIECES = [(i, 0, UNITS) for i in range(12)] + [(i, unit, 1) for i in range(12, 16) for unit in range(UNITS)]
 WAYS = "BCAACABBBBABABBBCBAAABBB"
 ORDER = (
-    0, 1, 2, 3, 4, 5, 6, 101, 102, 100, 103, 7, 107, 106, 104, 8, 9, 10, 11, 105, 12, 13, 14, 15,
+    101, 102, 0, 1, 100, 103, 2, 3, 4, 5, 6, 7, 107, 106, 104, 8, 9, 10, 11, 105, 12, 13, 14, 15,
     16, 17, 18, 108, 19, 20, 21, 22, 110, 202, 200, 201, 122, 116, 203, 207, 111, 204, 205, 301, 23, 206, 109, 302,
     210, 120, 208, 113, 216, 304, 222, 123, 300, 402, 24, 303, 307, 114, 316, 401, 119, 211, 121, 305, 306, 403, 220, 115,
     112, 209, 310, 405, 308, 213, 400, 117, 404, 322, 223, 416, 407, 410, 502, 118, 219, 406, 500, 214, 320, 507, 501, 311,
@@ -187,10 +187,6 @@
         return jnp.concatenate([m.ring[UNITS * slot + unit].reshape(D, LANES) for unit in range(UNITS)], axis=1)
 
     fetch_units(lambda i: m.h_qkv6.at[:, :, :, :, i * LANES : (i + 1) * LANES], 0, 18, m.w_sem.at[6])
-    for i, (name, src, dst) in enumerate(order):
-        copies[name] = pltpu.make_async_copy(src, dst, m.w_sem.at[i])
-        copies[name].start()
-    fetch_units(lambda i: m.h_fo.at[i // 6, :, :, :, :, i % 6 * LANES : (i % 6 + 1) * LANES], 24, 24, m.w_sem.at[7])
     if net:
         net.greet()
 
@@ -227,6 +223,10 @@
             got = got + m.self_bias[bias : bias + 1, cols]
         got = got.astype(BF)
         ref[:, cols] = got * scale if bias == 0 else got
+    for i, (name, src, dst) in enumerate(order):
+        copies[name] = pltpu.make_async_copy(src, dst, m.w_sem.at[i])
+        copies[name].start()
+    fetch_units(lambda i: m.h_fo.at[i // 6, :, :, :, :, i % 6 * LANES : (i % 6 + 1) * LANES], 24, 24, m.w_sem.at[7])
     m.vt[...] = m.v[...].T
     attend(m.q, m.k, m.vt, m.bias_s, m.p_s, xt.at[R_SMIX : R_SMIX + D])
     m.vt[...] = m.k[...].T * scale

time: 115 us -> 113 us (0.983)
  Pallas kernels: 113 us -> 111 us
    pallas_call x1, Pallas kernels: 108 us -> 106 us  [run_sum(): pl.pallas_call(functools.partial(sum_kernel, INPUTS + SUM_OUT + list(tabl...]
where the time goes in v4:
time: 113 us
  Pallas kernels  111 us (98%)
  between operations  1.5 us (1%)
    pallas_call x1, Pallas kernels, run_sum(): pl.pallas_call(functools.partial(sum_kernel, INPUTS + SUM_OUT + list(tabl...  106 us
    pallas_call x1, Pallas kernels, place(): pl.pallas_call(place_kernel, out_shape=(jax.ShapeDtypeStruct(result.shape...  4.73 us

profile of v4, /device:TPU:0, one launch (start us, length us, event | category | flops | bytes accessed | tf_op | source)
XLA Modules:
  0.0 112.7 jit_solution(17159453216452578944)
XLA Ops:
  1.3 106.5 %shard_map.374 = (bf16[256,768]{1,0:T(8,128)(2,1)}, f32[256,768]{1,0:T(8,128)}, bf16[48,2,2,48,128]{4,3,2,1,0:T(8,128)(2,1)}, f32[16,768]{1,0:T(8,128)}, f32[24,128]{1,0:T(8,128)}) custom-call(bf16[256,768]{1,0:T(8,128)(2,1)} %bitcast.19, bf16[16,768]{1,0:T(8,128)(2,1)} %bitcast.25, s32[64,256]{1,0:T(8,128)} %bitcast.22, s32[64,256]{1,0:T(8,128)} %bitcast.23, ...), custom_call_target="tpu_custom_call" | custom-call | flops 15000000512 | bytes 50000000 | tf_op jit(solution)/shard_map/pallas_call | solution.py:877
  107.8 4.7 %shard_map.375 = (bf16[256,768]{1,0:T(8,128)(2,1)}, f32[256,768]{1,0:T(8,128)}, f32[16,768]{1,0:T(8,128)}, f32[96,2304]{1,0:T(8,128)}, f32[2,96]{1,0:T(2,128)}, ...) custom-call(bf16[256,768]{1,0:T(8,128)(2,1)} %get-tuple-element.45.r, ...), custom_call_target="tpu_custom_call" | custom-call | tf_op jit(solution)/shard_map/pallas_call | solution.py:916
